TPU v7x, 32 devices: a whole 2x2x4 slice. The times are simulated.
32 devices in a mesh: section: 2 (over x), fsdp: 4 (over z), tensor: 4 (over y, core).
Axes of the slice: x: 2, y: 2, z: 4, core: 2. Of those that a mesh axis runs over, the one named last changes fastest.
Arguments:
- tokens: bfloat16 [8192, 768], P('fsdp'), may hold values from -6 to 6
- segment_ids: int32 [8, 1024], P('fsdp'), may hold values from 0 to 5, never falling along the last dimension, each value on 1 to 512 neighbouring positions
- ln_gain: bfloat16 [2, 2, 768], P('section', None, 'fsdp'), may hold values from 0.5 to 1.5
- ln_bias: bfloat16 [2, 2, 768], P('section', None, 'fsdp'), may hold values from -1.75 to 1.75
- w_qkv: bfloat16 [2, 768, 3, 768], P('section', 'fsdp', None, 'tensor'), may hold values from -0.21875 to 0.21875
- b_qkv: bfloat16 [2, 3, 768], P('section', None, 'tensor'), may hold values from -3 to 3
- w_o: bfloat16 [2, 768, 768], P('section', 'tensor', 'fsdp'), may hold values from -0.875 to 0.875
- b_o: bfloat16 [2, 768], P('section', 'fsdp'), may hold values from -1.75 to 1.75
- w_in: bfloat16 [2, 768, 3072], P('section', 'fsdp', 'tensor'), may hold values from -0.21875 to 0.21875
- b_in: bfloat16 [2, 3072], P('section', 'tensor'), may hold values from -3 to 3
- w_out: bfloat16 [2, 3072, 768], P('section', 'tensor', 'fsdp'), may hold values from -0.109375 to 0.109375
- b_out: bfloat16 [2, 768], P('section', 'fsdp'), may hold values from -1.75 to 1.75
- cotangent: bfloat16 [8192, 768], P('fsdp'), may hold values from -6 to 6
Outputs:
- layer_out: bfloat16 [2, 8192, 768], P('section', 'fsdp')
- input_grad: bfloat16 [2, 8192, 768], P('section', 'fsdp')
- grad_ln_gain: float32 [2, 2, 768], P('section', None, 'fsdp')
- grad_ln_bias: float32 [2, 2, 768], P('section', None, 'fsdp')
- grad_w_qkv: float32 [2, 768, 3, 768], P('section', 'fsdp', None, 'tensor')
- grad_b_qkv: float32 [2, 3, 768], P('section', None, 'tensor')
- grad_w_o: float32 [2, 768, 768], P('section', 'tensor', 'fsdp')
- grad_b_o: float32 [2, 768], P('section', 'fsdp')
- grad_w_in: float32 [2, 768, 3072], P('section', 'fsdp', 'tensor')
- grad_b_in: float32 [2, 3072], P('section', 'tensor')
- grad_w_out: float32 [2, 3072, 768], P('section', 'tensor', 'fsdp')
- grad_b_out: float32 [2, 768], P('section', 'fsdp')
Inputs may be any that keep to these rules, and one draw needn't show every extreme that they name: `segment_ids`: along each sequence the ids never fall; each of the 6 documents has 1 to 512 tokens, and one has exactly 512.
All inputs are finite; a program needn't handle non-finite values.
Results may differ from a plain program's by a relative error of at most 0.023.
Values may be sent and summed in bfloat16 or wider, within the bound.
A program may use at most 256 MiB of HBM per device.

v0:
```python
import math

import jax
import jax.numpy as jnp
from jax import lax
from jax.sharding import PartitionSpec as P

HEAD = 64


eps_norm = 1e-05


def from_behind(block, axis, distance):
    devices = range(lax.axis_size(axis))
    route = [(i - distance, i) for i in devices if i - distance in devices]
    return lax.ppermute(block, axis, route)


def norm_pair(row_data, gain_rows, shift_rows):
    row_mean = jnp.mean(row_data, axis=-1, keepdims=True)
    centred = row_data - row_mean
    row_var = jnp.mean(centred * centred, axis=-1, keepdims=True)
    scaled = centred * lax.rsqrt(row_var + eps_norm)
    return (scaled * gain_rows[0] + shift_rows[0], scaled * gain_rows[1] + shift_rows[1])


def positions_within(segment):
    positions = jnp.arange(segment.shape[0], dtype=jnp.int32)
    starts = jnp.concatenate([jnp.ones((1,), jnp.bool_), segment[1:] != segment[:-1]])
    first_row = lax.cummax(jnp.where(starts, positions, jnp.zeros_like(positions)), axis=0)
    return (positions - first_row).astype(jnp.float32)


def rotary_tables(segment, head_size):
    half_width = head_size // 8
    freq_table = 10000.0 ** (-2.0 * jnp.arange(half_width, dtype=jnp.float32) / (head_size // 4))
    angle_table = positions_within(segment)[:, None] * freq_table[None, :]
    cos_table = jnp.concatenate([jnp.cos(angle_table), jnp.cos(angle_table)], axis=-1)
    sine_table = jnp.concatenate([jnp.sin(angle_table), jnp.sin(angle_table)], axis=-1)
    return (cos_table, sine_table)


def rotate(vectors, cos_table, sine_table):
    rot_width = cos_table.shape[-1]
    part_rot = vectors[..., :rot_width]
    lower_half = part_rot[..., : rot_width // 2]
    upper_half = part_rot[..., rot_width // 2 :]
    turned = jnp.concatenate([-upper_half, lower_half], axis=-1)
    rotated = part_rot * cos_table[:, None, :] + turned * sine_table[:, None, :]
    return jnp.concatenate([rotated, vectors[..., rot_width:]], axis=-1)


def exact_gelu(pre_active):
    return jax.nn.gelu(pre_active, approximate=False)


def block_softmax(query_blk, key_heads, segment, start_row):
    scores = jnp.einsum("qhe,khe->hqk", query_blk, key_heads, preferred_element_type=jnp.float32)
    row_ids = start_row + jnp.arange(query_blk.shape[0], dtype=jnp.int32)
    col_ids = jnp.arange(key_heads.shape[0], dtype=jnp.int32)
    seg_blk = segment[start_row : start_row + query_blk.shape[0]]
    allowed = (col_ids[None, :] <= row_ids[:, None]) & (seg_blk[:, None] == segment[None, :])
    scores = jnp.where(allowed[None], scores, -1000000000.0)
    row_max = jnp.max(scores, axis=-1, keepdims=True)
    expont = jnp.exp(scores - row_max)
    return expont / jnp.sum(expont, axis=-1, keepdims=True)


def attend(query_heads, key_heads, values, segment):
    length = query_heads.shape[0]
    block_rows = min(512, length)
    out_parts = []
    for start_row in range(0, length, block_rows):
        softmax_w = block_softmax(
            query_heads[start_row : start_row + block_rows], key_heads, segment, start_row
        )
        out_parts.append(
            jnp.einsum(
                "hqk,khe->qhe",
                softmax_w.astype(jnp.bfloat16),
                values,
                preferred_element_type=jnp.float32,
            )
        )
    return jnp.concatenate(out_parts, axis=0)


def attend_back(query_heads, key_heads, values, grad_mix, segment):
    length = query_heads.shape[0]
    block_rows = min(512, length)
    grad_keys = jnp.zeros(key_heads.shape, jnp.float32)
    grad_values = jnp.zeros(values.shape, jnp.float32)
    grad_parts = []
    for start_row in range(0, length, block_rows):
        query_blk = query_heads[start_row : start_row + block_rows]
        grad_blk = grad_mix[start_row : start_row + block_rows]
        softmax_w = block_softmax(query_blk, key_heads, segment, start_row)
        softmax_b = softmax_w.astype(jnp.bfloat16)
        grad_probs = jnp.einsum(
            "qhe,khe->hqk", grad_blk, values, preferred_element_type=jnp.float32
        )
        grad_scores = (
            softmax_w * (grad_probs - jnp.sum(softmax_w * grad_probs, axis=-1, keepdims=True))
        ).astype(jnp.bfloat16)
        grad_parts.append(
            jnp.einsum("hqk,khe->qhe", grad_scores, key_heads, preferred_element_type=jnp.float32)
        )
        grad_keys = grad_keys + jnp.einsum(
            "hqk,qhe->khe", grad_scores, query_blk, preferred_element_type=jnp.float32
        )
        grad_values = grad_values + jnp.einsum(
            "hqk,qhe->khe", softmax_b, grad_blk, preferred_element_type=jnp.float32
        )
    return (jnp.concatenate(grad_parts, axis=0), grad_keys, grad_values)


def turn_heads(query_pre, key_pre, cos_table, sine_table):
    return (
        rotate(query_pre, cos_table, sine_table) * (1.0 / math.sqrt(HEAD)),
        rotate(key_pre, cos_table, sine_table),
    )


def forward_part(rows_b, segment, gathered, local_bias):
    gain_rows, shift_rows, w_qkv, w_o, b_o, w_in, w_out, b_out = gathered
    length = rows_b.shape[0]
    h_one, h_two = norm_pair(
        rows_b.astype(jnp.float32), gain_rows.astype(jnp.float32), shift_rows.astype(jnp.float32)
    )
    h_one_b = h_one.astype(jnp.bfloat16)
    h_two_b = h_two.astype(jnp.bfloat16)
    joined_qkv = (
        jnp.einsum("rd,dsc->rsc", h_one_b, w_qkv, preferred_element_type=jnp.float32)
        + local_bias[0][None]
    )
    cos_table, sine_table = rotary_tables(segment, HEAD)
    query_heads, key_heads = turn_heads(
        joined_qkv[:, 0].reshape(length, -1, HEAD),
        joined_qkv[:, 1].reshape(length, -1, HEAD),
        cos_table,
        sine_table,
    )
    values = joined_qkv[:, 2].reshape(length, -1, HEAD).astype(jnp.bfloat16)
    head_mix = attend(
        query_heads.astype(jnp.bfloat16), key_heads.astype(jnp.bfloat16), values, segment
    )
    head_mix = head_mix.reshape(length, -1).astype(jnp.bfloat16)
    pre_active = jnp.dot(h_two_b, w_in, preferred_element_type=jnp.float32) + local_bias[1]
    active = exact_gelu(pre_active).astype(jnp.bfloat16)
    return jnp.dot(head_mix, w_o, preferred_element_type=jnp.float32) + jnp.dot(
        active, w_out, preferred_element_type=jnp.float32
    )


def backward_local(rows_b, upstream, segment, gathered, local_bias):
    gain_rows, shift_rows, w_qkv, w_o, b_o, w_in, w_out, b_out = gathered
    length = rows_b.shape[0]
    (h_one, h_two), norm_back = jax.vjp(
        norm_pair,
        rows_b.astype(jnp.float32),
        gain_rows.astype(jnp.float32),
        shift_rows.astype(jnp.float32),
    )
    h_one_b = h_one.astype(jnp.bfloat16)
    h_two_b = h_two.astype(jnp.bfloat16)
    joined_qkv = (
        jnp.einsum("rd,dsc->rsc", h_one_b, w_qkv, preferred_element_type=jnp.float32)
        + local_bias[0][None]
    )
    cos_table, sine_table = rotary_tables(segment, HEAD)

    def turn_local(query_pre, key_pre):
        return turn_heads(query_pre, key_pre, cos_table, sine_table)

    (query_heads, key_heads), turn_back = jax.vjp(
        turn_local,
        joined_qkv[:, 0].reshape(length, -1, HEAD),
        joined_qkv[:, 1].reshape(length, -1, HEAD),
    )
    query_b = query_heads.astype(jnp.bfloat16)
    keys_b = key_heads.astype(jnp.bfloat16)
    values_b = joined_qkv[:, 2].reshape(length, -1, HEAD).astype(jnp.bfloat16)
    head_mix = attend(query_b, keys_b, values_b, segment).reshape(length, -1).astype(jnp.bfloat16)
    pre_active = jnp.dot(h_two_b, w_in, preferred_element_type=jnp.float32) + local_bias[1]
    active, gelu_back = jax.vjp(exact_gelu, pre_active)
    active_b = active.astype(jnp.bfloat16)
    upstream_f = upstream.astype(jnp.float32)
    grad_outbias = jnp.sum(upstream_f, axis=0)
    grad_wo = jnp.einsum("rc,rd->cd", head_mix, upstream, preferred_element_type=jnp.float32)
    grad_wout = jnp.einsum("rf,rd->fd", active_b, upstream, preferred_element_type=jnp.float32)
    grad_mix = (
        jnp.einsum("rd,cd->rc", upstream, w_o, preferred_element_type=jnp.float32)
        .astype(jnp.bfloat16)
        .reshape(length, -1, HEAD)
    )
    grad_inner = gelu_back(
        jnp.einsum("rd,fd->rf", upstream, w_out, preferred_element_type=jnp.float32)
    )[0].astype(jnp.bfloat16)
    grad_bin = jnp.sum(grad_inner.astype(jnp.float32), axis=0)
    grad_win = jnp.einsum("rd,rf->df", h_two_b, grad_inner, preferred_element_type=jnp.float32)
    grad_two = jnp.einsum("rf,df->rd", grad_inner, w_in, preferred_element_type=jnp.float32)
    grad_query, grad_keys, grad_values = attend_back(query_b, keys_b, values_b, grad_mix, segment)
    grad_qpre, grad_kpre = turn_back((grad_query, grad_keys))
    grad_joined = jnp.stack(
        [
            grad_qpre.reshape(length, -1),
            grad_kpre.reshape(length, -1),
            grad_values.reshape(length, -1),
        ],
        axis=1,
    ).astype(jnp.bfloat16)
    grad_bqkv = jnp.sum(grad_joined.astype(jnp.float32), axis=0)
    grad_wqkv = jnp.einsum("rd,rsc->dsc", h_one_b, grad_joined, preferred_element_type=jnp.float32)
    grad_one = jnp.einsum("rsc,dsc->rd", grad_joined, w_qkv, preferred_element_type=jnp.float32)
    grad_rows, grad_gains, grad_shifts = norm_back((grad_one, grad_two))
    grad_rows = lax.psum(grad_rows.astype(jnp.bfloat16), "tensor").astype(jnp.float32)
    grad_terms = (
        grad_gains,
        grad_shifts,
        grad_wqkv,
        grad_wo,
        grad_outbias,
        grad_win,
        grad_wout,
        grad_bqkv,
        grad_bin,
    )
    return (upstream_f + grad_rows, grad_terms)


def fetch_each(shards):
    return (
        lax.all_gather(shards[0], "fsdp", axis=1, tiled=True),
        lax.all_gather(shards[1], "fsdp", axis=1, tiled=True),
        lax.all_gather(shards[2], "fsdp", axis=0, tiled=True),
        lax.all_gather(shards[3], "fsdp", axis=1, tiled=True),
        lax.all_gather(shards[4], "fsdp", axis=0, tiled=True),
        lax.all_gather(shards[5], "fsdp", axis=0, tiled=True),
        lax.all_gather(shards[6], "fsdp", axis=1, tiled=True),
        lax.all_gather(shards[7], "fsdp", axis=0, tiled=True),
    )


def per_device(
    tokens,
    segment_ids,
    ln_gain,
    ln_bias,
    w_qkv,
    b_qkv,
    w_o,
    b_o,
    w_in,
    b_in,
    w_out,
    b_out,
    cotangent,
):
    seq_len = segment_ids.shape[1]
    micro_count = segment_ids.shape[0]
    width = tokens.shape[1]
    section_index = lax.axis_index("section")
    at_first = section_index == 0
    shards = (ln_gain[0], ln_bias[0], w_qkv[0], w_o[0], b_o[0], w_in[0], w_out[0], b_out[0])
    local_bias = (b_qkv[0].astype(jnp.float32), b_in[0].astype(jnp.float32))
    outputs = jnp.zeros((micro_count * seq_len, width), jnp.bfloat16)
    saved_inputs = jnp.zeros((micro_count, seq_len, width), jnp.bfloat16)
    arriving = jnp.zeros((seq_len, width), jnp.bfloat16)
    for step_index in range(micro_count + 1):
        gathered = fetch_each(shards)
        micro_index = step_index - section_index
        is_live = (micro_index >= 0) & (micro_index < micro_count)
        slot_index = jnp.clip(micro_index, 0, micro_count - 1)
        own_slot = min(step_index, micro_count - 1)
        own_rows = tokens[own_slot * seq_len : (own_slot + 1) * seq_len]
        rows_b = jnp.where(at_first, own_rows, arriving)
        segment = lax.dynamic_index_in_dim(segment_ids, slot_index, 0, keepdims=False)
        partial_sum = forward_part(rows_b, segment, gathered, local_bias)
        summed = lax.psum(partial_sum.astype(jnp.bfloat16), "tensor").astype(jnp.float32)
        result_b = (
            rows_b.astype(jnp.float32)
            + summed
            + gathered[4].astype(jnp.float32)
            + gathered[7].astype(jnp.float32)
        ).astype(jnp.bfloat16)
        current = lax.dynamic_slice_in_dim(outputs, slot_index * seq_len, seq_len, 0)
        outputs = lax.dynamic_update_slice_in_dim(
            outputs, jnp.where(is_live, result_b, current), slot_index * seq_len, 0
        )
        stored = lax.dynamic_index_in_dim(saved_inputs, slot_index, 0, keepdims=False)
        saved_inputs = lax.dynamic_update_index_in_dim(
            saved_inputs, jnp.where(is_live, rows_b, stored), slot_index, 0
        )
        if step_index < micro_count:
            arriving = from_behind(result_b, "section", 1)
    input_grads = jnp.zeros((micro_count * seq_len, width), jnp.bfloat16)
    back_in = jnp.zeros((seq_len, width), jnp.bfloat16)
    totals = None
    for turn_index in range(micro_count + 1):
        gathered = fetch_each(shards)
        micro_index = micro_count - 1 - turn_index + (1 - section_index)
        is_live = (micro_index >= 0) & (micro_index < micro_count)
        slot_index = jnp.clip(micro_index, 0, micro_count - 1)
        rows_b = lax.dynamic_index_in_dim(saved_inputs, slot_index, 0, keepdims=False)
        incoming = lax.dynamic_slice_in_dim(cotangent, slot_index * seq_len, seq_len, 0)
        upstream = jnp.where(at_first, back_in, incoming)
        segment = lax.dynamic_index_in_dim(segment_ids, slot_index, 0, keepdims=False)
        grad_rows, grad_terms = backward_local(rows_b, upstream, segment, gathered, local_bias)
        masked = tuple((jnp.where(is_live, term, jnp.zeros_like(term)) for term in grad_terms))
        totals = (
            masked
            if totals is None
            else tuple((left + right for left, right in zip(totals, masked)))
        )
        grad_b = grad_rows.astype(jnp.bfloat16)
        current = lax.dynamic_slice_in_dim(input_grads, slot_index * seq_len, seq_len, 0)
        input_grads = lax.dynamic_update_slice_in_dim(
            input_grads, jnp.where(is_live, grad_b, current), slot_index * seq_len, 0
        )
        if turn_index < micro_count:
            back_in = from_behind(grad_b, "section", -1)
    (
        grad_gains,
        grad_shifts,
        grad_wqkv,
        grad_wo,
        grad_outbias,
        grad_win,
        grad_wout,
        grad_bqkv,
        grad_bin,
    ) = totals
    norm_sums = lax.psum((grad_gains, grad_shifts), ("fsdp", "tensor"))
    piece_len = ln_gain.shape[2]
    first_col = lax.axis_index("fsdp") * piece_len
    gain_grad = lax.dynamic_slice_in_dim(norm_sums[0], first_col, piece_len, 1)
    shift_grad = lax.dynamic_slice_in_dim(norm_sums[1], first_col, piece_len, 1)
    weight_sums = (
        lax.psum_scatter(
            grad_wqkv.astype(jnp.bfloat16), "fsdp", scatter_dimension=0, tiled=True
        ).astype(jnp.float32),
        lax.psum_scatter(
            grad_wo.astype(jnp.bfloat16), "fsdp", scatter_dimension=1, tiled=True
        ).astype(jnp.float32),
        lax.psum_scatter(
            grad_outbias.astype(jnp.bfloat16), "fsdp", scatter_dimension=0, tiled=True
        ).astype(jnp.float32),
        lax.psum_scatter(
            grad_win.astype(jnp.bfloat16), "fsdp", scatter_dimension=0, tiled=True
        ).astype(jnp.float32),
        lax.psum_scatter(
            grad_wout.astype(jnp.bfloat16), "fsdp", scatter_dimension=1, tiled=True
        ).astype(jnp.float32),
    )
    bias_sums = lax.psum((grad_bqkv, grad_bin), "fsdp")
    return (
        outputs[None],
        input_grads[None],
        gain_grad[None],
        shift_grad[None],
        weight_sums[0][None],
        bias_sums[0][None],
        weight_sums[1][None],
        weight_sums[2][None],
        weight_sums[3][None],
        bias_sums[1][None],
        weight_sums[4][None],
        weight_sums[2][None],
    )


def solution(mesh):
    in_specs = (
        P("fsdp", None),
        P("fsdp", None),
        P("section", None, "fsdp"),
        P("section", None, "fsdp"),
        P("section", "fsdp", None, "tensor"),
        P("section", None, "tensor"),
        P("section", "tensor", "fsdp"),
        P("section", "fsdp"),
        P("section", "fsdp", "tensor"),
        P("section", "tensor"),
        P("section", "tensor", "fsdp"),
        P("section", "fsdp"),
        P("fsdp", None),
    )
    out_specs = (
        P("section", "fsdp", None),
        P("section", "fsdp", None),
        P("section", None, "fsdp"),
        P("section", None, "fsdp"),
        P("section", "fsdp", None, "tensor"),
        P("section", None, "tensor"),
        P("section", "tensor", "fsdp"),
        P("section", "fsdp"),
        P("section", "fsdp", "tensor"),
        P("section", "tensor"),
        P("section", "tensor", "fsdp"),
        P("section", "fsdp"),
    )
    return jax.shard_map(
        per_device, mesh=mesh, in_specs=in_specs, out_specs=out_specs, check_vma=False
    )
```

profile of v0, /device:TPU:0, one launch (start us, length us, event | category | flops | bytes accessed | tf_op | source)
XLA Modules:
  0.0 927.8 jit_solution(18338650687036371380)
XLA Ops:
  14.3 20.8 %all-gather.1 = bf16[1,2,768]{1,0,2:T(2,128)(2,1)S(1)} all-gather(bf16[1,2,192]{1,0,2:T(2,128)(2,1)S(1)} %copy.54), channel_id=3, replica_groups=mesh['section'=2,'fsdp'=4,'tensor'=4] {'fsdp'}, dimensions={2}, use_global_device_ids=true | all-gather | bytes 3840 | tf_op jit(solution)/shard_map/all_gather | solution.py:235
  35.6 5.2 slice_reduce_fusion.2
  40.8 16.7 %all-gather = bf16[1,2,768]{1,0,2:T(2,128)(2,1)S(1)} all-gather(bf16[1,2,192]{1,0,2:T(2,128)(2,1)S(1)} %copy.53), channel_id=2, replica_groups=mesh['section'=2,'fsdp'=4,'tensor'=4] {'fsdp'}, dimensions={2}, use_global_device_ids=true | all-gather | bytes 3840 | tf_op jit(solution)/shard_map/all_gather | solution.py:234
  57.9 4.6 slice_reduce_fusion.3
  62.8 44.2 %all-gather.2 = bf16[1,768,3,192]{3,2,0,1:T(4,128)(2,1)} all-gather(bf16[1,192,3,192]{3,2,0,1:T(4,128)(2,1)S(1)} %copy.55), channel_id=4, replica_groups=mesh['section'=2,'fsdp'=4,'tensor'=4] {'fsdp'}, dimensions={1}, use_global_device_ids=true | all-gather | bytes 1105920 | tf_op jit(solution)/shard_map/all_gather | solution.py:236
  107.0 3.4 copy.56
  121.8 18.2 %all-gather.3 = bf16[1,192,768]{1,0,2:T(2,128)(2,1)} all-gather(bf16[1,192,192]{1,0,2:T(2,128)(2,1)S(1)} %copy.57), channel_id=5, replica_groups=mesh['section'=2,'fsdp'=4,'tensor'=4] {'fsdp'}, dimensions={2}, use_global_device_ids=true | all-gather | bytes 368640 | tf_op jit(solution)/shard_map/all_gather | solution.py:237
  148.6 6.8 fusion.725
  155.3 6.1 fusion.730
  161.4 4.2 fusion.414
  168.3 12.6 %fusion.322 = f32[1024,768]{1,0:T(8,128)} fusion(f32[768]{0:T(1024)S(1)} %convert_reduce_fusion.15, f32[768]{0:T(1024)S(1)} %copy-done.186, f32[768]{0:T(1024)S(1)} %get-tuple-element.81, f32[1024]{0:T(1024)S(1)} %copy-done.208, f32[1024]{0:T(1024)S(1)} %copy-done.163, bf16[1,768,768]{1,2,0:T(8,128)(2,1)} %all-gather.13.cloned.1.call-done, ...), kind=kOutput, calls=%fused_computation.454 | convolution fusion | flops 2473328640 | bytes 7098369 | tf_op jit(solution)/shard_map/dot_general | solution.py:151
  180.9 3.8 add_convert_fusion.8
  186.6 9.6 %all-reduce.42 = (bf16[768]{0:T(1024)(128)(2,1)S(1)}, bf16[768]{0:T(1024)(128)(2,1)S(1)}) all-reduce(bf16[768]{0:T(1024)(128)(2,1)S(1)} %dynamic-update-slice.1, bf16[768]{0:T(1024)(128)(2,1)S(1)} %dynamic-update-slice), channel_id=9, replica_groups=mesh['section'=2,'fsdp'=4,'tensor'=4] {'fsdp'}, use_global_device_ids=true, to_apply=%add.37 | all-reduce | flops 1536 | bytes 6144
  196.3 30.1 %all-reduce.49.cloned.1.call-done = bf16[1024,768]{1,0:T(8,128)(2,1)} async-done(((bf16[1024,768]{1,0:T(8,128)(2,1)}), bf16[1024,768]{1,0:T(8,128)(2,1)}) %all-reduce.49.cloned.1.call-update) | async-done | bytes 1572880 | tf_op jit(solution)/shard_map/psum | solution.py:280
  230.9 4.5 collective-permute-start
  237.8 3.0 fusion.222
  240.9 27.2 %collective-permute-done = bf16[1024,768]{1,0:T(8,128)(2,1)} collective-permute-done((bf16[1024,768]{1,0:T(8,128)(2,1)}, bf16[1024,768]{1,0:T(8,128)(2,1)}, u32[]{:S(2)}, u32[]{:S(2)}) %collective-permute-start) | collective-permute-done | bytes 1572896 | tf_op jit(solution)/shard_map/ppermute | solution.py:17
  275.4 6.7 fusion.735
  282.1 6.7 fusion.740
  288.9 4.1 fusion.416
  295.7 12.9 %fusion.319 = f32[1024,768]{1,0:T(8,128)} fusion(bf16[1024,768]{1,0:T(8,128)(2,1)} %copy-done.3, f32[1024]{0:T(1024)S(1)} %copy-done.210, f32[1024]{0:T(1024)S(1)} %copy-done.167, f32[768]{0:T(1024)S(1)} %convert_reduce_fusion.15, f32[768]{0:T(1024)S(1)} %copy-done.187, f32[768]{0:T(1024)S(1)} %get-tuple-element.81, ...), kind=kOutput, calls=%fused_computation.453 | convolution fusion | flops 2472542208 | bytes 7095296 | tf_op jit(solution)/shard_map/dot_general | solution.py:151
  308.6 3.8 add_convert_fusion.7
  312.5 45.7 %all-reduce.51.cloned.1.call-done = bf16[1024,768]{1,0:T(8,128)(2,1)} async-done(((bf16[1024,768]{1,0:T(8,128)(2,1)}), bf16[1024,768]{1,0:T(8,128)(2,1)}) %all-reduce.51.cloned.1.call-update) | async-done | bytes 1572880 | tf_op jit(solution)/shard_map/psum | solution.py:280
  358.2 4.9 select_dynamic-update-slice_fusion.2
  363.0 4.9 collective-permute-start.1
  371.2 29.1 %collective-permute-done.1 = bf16[1024,768]{1,0:T(8,128)(2,1)} collective-permute-done((bf16[1024,768]{1,0:T(8,128)(2,1)}, bf16[1024,768]{1,0:T(8,128)(2,1)}, u32[]{:S(2)}, u32[]{:S(2)}) %collective-permute-start.1) | collective-permute-done | bytes 1572896 | tf_op jit(solution)/shard_map/ppermute | solution.py:17
  413.4 6.8 fusion.745
  420.2 6.7 fusion.750
  428.8 6.7 fusion.755
  435.5 6.6 fusion.760
  442.1 4.8 fusion.410
  463.7 7.7 fusion.147
  471.4 3.3 convert_reduce_fusion.11
  474.8 5.4 fusion.89
  490.7 6.6 fusion.765
  497.2 6.7 fusion.770
  504.6 3.7 fusion.712
  510.1 4.2 fusion.418
  514.4 4.1 fusion.417
  528.2 16.1 %fusion.148 = (f32[1024,768]{1,0:T(8,128)}, f32[1024,768]{1,0:T(8,128)}, f32[1024,768]{1,0:T(8,128)}) fusion(f32[768]{0:T(1024)S(1)} %convert_reduce_fusion.15, f32[1024,768]{1,0:T(8,128)S(1)} %fusion.353, bf16[1,768,768]{2,1,0:T(8,128)(2,1)S(1)} %copy-done.219, f32[1024]{0:T(1024)S(1)} %copy-done.156, f32[1024]{0:T(1024)S(1)} %copy-done.147, ...), kind=kOutput, calls=%fused_computation.196 | convolution fusion | flops 1311768576 | bytes 15355908 | tf_op jit(solution)/shard_map/dot_general | solution.py:185
  544.3 6.6 fusion.775
  551.0 6.5 fusion.780
  560.6 3.8 select_dynamic-update-slice_fusion.1
  565.9 12.7 %fusion.316 = f32[1024,768]{1,0:T(8,128)} fusion(bf16[1024,768]{1,0:T(8,128)(2,1)} %copy-done.4, f32[1024]{0:T(1024)S(1)} %copy-done.206, f32[1024]{0:T(1024)S(1)} %copy-done.161, f32[768]{0:T(1024)S(1)} %convert_reduce_fusion.15, f32[768]{0:T(1024)S(1)} %copy-done.190, f32[768]{0:T(1024)S(1)} %get-tuple-element.81, ...), kind=kOutput, calls=%fused_computation.452 | convolution fusion | flops 2472542208 | bytes 7095296 | tf_op jit(solution)/shard_map/dot_general | solution.py:151
  578.5 24.6 %collective-permute-done.2 = bf16[1024,768]{1,0:T(8,128)(2,1)} collective-permute-done((bf16[1024,768]{1,0:T(8,128)(2,1)}, bf16[1024,768]{1,0:T(8,128)(2,1)}, u32[]{:S(2)}, u32[]{:S(2)}) %collective-permute-start.2) | collective-permute-done | bytes 1572896 | tf_op jit(solution)/shard_map/ppermute | solution.py:17
  603.2 3.1 convert_reduce_fusion.6
  607.1 4.2 multiply_reduce_fusion.3
  635.1 4.6 fusion.395
  639.7 38.0 %all-reduce.55.cloned.1.call-done = bf16[1024,768]{1,0:T(8,128)(2,1)} async-done(((bf16[1024,768]{1,0:T(8,128)(2,1)}), bf16[1024,768]{1,0:T(8,128)(2,1)}) %all-reduce.55.cloned.1.call-update) | async-done | bytes 1572880 | tf_op jit(solution)/shard_map/psum | solution.py:217
  677.8 4.1 select_dynamic-update-slice_fusion
  683.3 4.1 fusion.398
  691.6 28.2 %collective-permute-done.3 = bf16[1024,768]{1,0:T(8,128)(2,1)S(1)} collective-permute-done((bf16[1024,768]{1,0:T(8,128)(2,1)S(1)}, bf16[1024,768]{1,0:T(8,128)(2,1)S(1)}, u32[]{:S(2)}, u32[]{:S(2)}) %collective-permute-start.3) | collective-permute-done | bytes 1572896 | tf_op jit(solution)/shard_map/ppermute | solution.py:17
  736.6 3.9 fusion.324
  755.4 3.0 fusion.247
  763.6 4.9 fusion.225
  778.6 3.9 copy.94
  792.7 3.9 copy.95
  796.6 3.1 add_convert_fusion.10
  801.2 11.7 %all-reduce.38 = bf16[768]{0:T(1024)(128)(2,1)S(1)} all-reduce(bf16[768]{0:T(1024)(128)(2,1)S(1)} %add_convert_fusion.18), channel_id=12, replica_groups=mesh['section'=2,'fsdp'=4,'tensor'=4] {'fsdp'}, use_global_device_ids=true, to_apply=%region_83.84.clone | all-reduce | flops 768 | bytes 3072
  818.4 9.0 all-reduce.40
  828.9 59.7 %all-reduce.39 = (f32[2,768]{1,0:T(2,128)S(1)}, f32[2,768]{1,0:T(2,128)S(1)}) all-reduce(f32[2,768]{1,0:T(2,128)S(1)} %select_add_fusion.1, f32[2,768]{1,0:T(2,128)S(1)} %select_add_fusion), channel_id=1, replica_groups=mesh['section'=2,'fsdp'=4,'tensor'=4] {'fsdp','tensor'}, use_global_device_ids=true, to_apply=%region_66.67 | all-reduce | flops 3072 | bytes 24576 | tf_op jit(solution)/shard_map/psum | solution.py:334
  891.6 3.7 fusion.233
  895.4 3.4 fusion.230
  902.9 15.8 %reduce-scatter.11.cloned.1.call-done = bf16[192,768]{1,0:T(8,128)(2,1)} async-done(((bf16[768,768]{1,0:T(8,128)(2,1)}), bf16[192,768]{1,0:T(8,128)(2,1)}) %reduce-scatter.11.cloned.1.call-update) | async-done | bytes 294928 | tf_op jit(solution)/shard_map/reduce_scatter | solution.py:349
  (812 shorter events, 212.7 us)
Async XLA Ops:
  7.2 161.0 %all-gather.11.cloned.1.call-start = ((), (), s32[]{:S(2)}) async-start(), calls=%async_computation.10 | async-start | bytes 1474560 | tf_op jit(solution)/shard_map/all_gather | solution.py:239
  7.9 160.3 %all-gather.13.cloned.1.call-start = ((), (), s32[]{:S(2)}) async-start(), calls=%async_computation.11 | async-start | bytes 1474560 | tf_op jit(solution)/shard_map/all_gather | solution.py:240
  8.7 217.7 %all-reduce.49.cloned.1.call-start = ((), (), s32[]{:S(2)}) async-start(), calls=%async_computation.4 | async-start | bytes 3145728 | tf_op jit(solution)/shard_map/psum | solution.py:280
  11.8 50.7 %copy-start.110 = (bf16[1,192,3,192]{3,1,2,0:T(8,128)(2,1)S(1)}, bf16[1,192,3,192]{3,1,2,0:T(8,128)(2,1)}, u32[]{:S(2)}) copy-start(bf16[1,192,3,192]{3,1,2,0:T(8,128)(2,1)} %param.17) | copy-start | bytes 663556
  11.8 98.6 %copy-start.162 = (f32[1024]{0:T(1024)}, f32[1024]{0:T(1024)S(1)}, u32[]{:S(2)}) copy-start(f32[1024]{0:T(1024)S(1)} %broadcast_multiply_fusion.5) | copy-start | bytes 12292
  14.0 96.4 %copy-start.207 = (f32[1024]{0:T(1024)}, f32[1024]{0:T(1024)S(1)}, u32[]{:S(2)}) copy-start(f32[1024]{0:T(1024)S(1)} %add_rsqrt_fusion.2) | copy-start | bytes 12292
  40.8 69.6 %copy-start.192 = (f32[768]{0:T(1024)}, f32[768]{0:T(1024)S(1)}, u32[]{:S(2)}) copy-start(f32[768]{0:T(1024)S(1)} %get-tuple-element.82) | copy-start | bytes 9220
  57.9 52.5 %copy-start = (bf16[2048,768]{1,0:T(8,128)(2,1)S(1)}, bf16[2048,768]{1,0:T(8,128)(2,1)}, u32[]{:S(2)}) copy-start(bf16[2048,768]{1,0:T(8,128)(2,1)} %param.13) | copy-start | bytes 9437188
  62.5 442.1 %copy-start.122 = (f32[768]{0:T(1024)}, f32[768]{0:T(1024)S(1)}, u32[]{:S(2)}) copy-start(f32[768]{0:T(1024)S(1)} %get-tuple-element.80) | copy-start | bytes 9220
  113.9 7.6 copy-start.121
  121.6 33.7 %copy-start.66 = (f32[1024,16]{0,1:T(8,128)}, f32[1024,16]{0,1:T(8,128)S(1)}, u32[]{:S(2)}) copy-start(f32[1024,16]{0,1:T(8,128)S(1)} %pad_maximum_fusion.15) | copy-start | bytes 196612
  142.2 225.9 %copy-start.23 = (bf16[1,192,768]{2,1,0:T(8,128)(2,1)}, bf16[1,192,768]{2,1,0:T(8,128)(2,1)S(1)}, u32[]{:S(2)}) copy-start(bf16[1,192,768]{2,1,0:T(8,128)(2,1)S(1)} %copy.58) | copy-start | bytes 884740
  184.8 173.4 %all-reduce.51.cloned.1.call-start = ((), (), s32[]{:S(2)}) async-start(), calls=%async_computation.5 | async-start | bytes 3145728 | tf_op jit(solution)/shard_map/psum | solution.py:280
  196.2 34.7 %copy-start.124 = (f32[768]{0:T(1024)}, f32[768]{0:T(1024)S(1)}, u32[]{:S(2)}) copy-start(f32[768]{0:T(1024)S(1)} %convert_element_type.507) | copy-start | bytes 9220
  196.3 34.7 %copy-start.127 = (f32[768]{0:T(1024)}, f32[768]{0:T(1024)S(1)}, u32[]{:S(2)}) copy-start(f32[768]{0:T(1024)S(1)} %convert_element_type.506) | copy-start | bytes 9220
  230.9 37.2 %collective-permute-start = (bf16[1024,768]{1,0:T(8,128)(2,1)}, bf16[1024,768]{1,0:T(8,128)(2,1)}, u32[]{:S(2)}, u32[]{:S(2)}) collective-permute-start(bf16[1024,768]{1,0:T(8,128)(2,1)} %get-tuple-element.116), channel_id=1, source_target_pairs={{0,16},{1,17},{2,18},{3,19},{4,20},{5,21},{6,22},{7,23},{8,24},{9,... | collective-permute-start | bytes 4718600 | tf_op jit(solution)/shard_map/ppermute | solution.py:17
  235.5 38.4 %copy-start.74 = (f32[1024,16]{0,1:T(8,128)}, f32[1024,16]{0,1:T(8,128)S(1)}, u32[]{:S(2)}) copy-start(f32[1024,16]{0,1:T(8,128)S(1)} %pad_maximum_fusion.18) | copy-start | bytes 196612
  235.5 38.4 %copy-start.69 = (f32[1024,16]{0,1:T(8,128)}, f32[1024,16]{0,1:T(8,128)S(1)}, u32[]{:S(2)}) copy-start(f32[1024,16]{0,1:T(8,128)S(1)} %pad_maximum_fusion.17) | copy-start | bytes 196612
  237.6 30.5 %copy-start.1 = (bf16[2048,768]{1,0:T(8,128)(2,1)S(1)}, bf16[2048,768]{1,0:T(8,128)(2,1)}, u32[]{:S(2)}) copy-start(bf16[2048,768]{1,0:T(8,128)(2,1)} %param.13) | copy-start | bytes 9437188
  308.6 49.6 %copy-start.125 = (f32[768]{0:T(1024)S(1)}, f32[768]{0:T(1024)}, u32[]{:S(2)}) copy-start(f32[768]{0:T(1024)} %copy-done.124) | copy-start | bytes 9220
  308.6 49.6 %copy-start.128 = (f32[768]{0:T(1024)S(1)}, f32[768]{0:T(1024)}, u32[]{:S(2)}) copy-start(f32[768]{0:T(1024)} %copy-done.127) | copy-start | bytes 9220
  312.4 245.1 %all-reduce.53.cloned.1.call-start = ((), (), s32[]{:S(2)}) async-start(), calls=%async_computation.6 | async-start | bytes 3145728 | tf_op jit(solution)/shard_map/psum | solution.py:217
  358.2 9.8 %copy-start.118 = (f32[1024,8]{0,1:T(8,128)S(1)}, f32[1024,8]{0,1:T(8,128)}, u32[]{:S(2)}) copy-start(f32[1024,8]{0,1:T(8,128)} %get-tuple-element.205) | copy-start | bytes 98308
  358.2 9.8 %copy-start.117 = (f32[1024,8]{0,1:T(8,128)S(1)}, f32[1024,8]{0,1:T(8,128)}, u32[]{:S(2)}) copy-start(f32[1024,8]{0,1:T(8,128)} %get-tuple-element.206) | copy-start | bytes 98308
  363.0 37.2 %collective-permute-start.1 = (bf16[1024,768]{1,0:T(8,128)(2,1)}, bf16[1024,768]{1,0:T(8,128)(2,1)}, u32[]{:S(2)}, u32[]{:S(2)}) collective-permute-start(bf16[1024,768]{1,0:T(8,128)(2,1)} %get-tuple-element.114), channel_id=1, source_target_pairs={{0,16},{1,17},{2,18},{3,19},{4,20},{5,21},{6,22},{7,23},{8,24},{9,... | collective-permute-start | bytes 4718600 | tf_op jit(solution)/shard_map/ppermute | solution.py:17
  368.0 43.8 %copy-start.86 = (f32[1024,16]{0,1:T(8,128)}, f32[1024,16]{0,1:T(8,128)S(1)}, u32[]{:S(2)}) copy-start(f32[1024,16]{0,1:T(8,128)S(1)} %pad_maximum_fusion.19) | copy-start | bytes 196612
  368.0 43.7 %copy-start.88 = (f32[1024,16]{0,1:T(8,128)}, f32[1024,16]{0,1:T(8,128)S(1)}, u32[]{:S(2)}) copy-start(f32[1024,16]{0,1:T(8,128)S(1)} %pad_maximum_fusion.20) | copy-start | bytes 196612
  368.1 32.2 %copy-start.2 = (bf16[2048,768]{1,0:T(8,128)(2,1)S(1)}, bf16[2048,768]{1,0:T(8,128)(2,1)}, u32[]{:S(2)}) copy-start(bf16[2048,768]{1,0:T(8,128)(2,1)} %param.13) | copy-start | bytes 9437188
  442.1 9.5 %slice-start.12 = ((s8[6291456]{0:T(1024)(128)(4,1)}), s8[4194304]{0:T(1024)(128)(4,1)S(1)}, s32[]{:S(2)}) async-start(s8[6291456]{0:T(1024)(128)(4,1)} %bitcast.523), calls=%async_computation.27 | async-start | bytes 8388608
  459.7 23.0 %copy-start.141 = (f32[1024]{0:T(1024)}, f32[1024]{0:T(1024)S(1)}, u32[]{:S(2)}) copy-start(f32[1024]{0:T(1024)S(1)} %broadcast_multiply_fusion) | copy-start | bytes 12292
  459.7 20.5 %copy-start.146 = (f32[1024]{0:T(1024)}, f32[1024]{0:T(1024)S(1)}, u32[]{:S(2)}) copy-start(f32[1024]{0:T(1024)S(1)} %broadcast_multiply_fusion.1) | copy-start | bytes 12292
  463.7 11.1 %copy-start.37 = (f32[1024,768,1]{1,0,2:T(8,128)}, f32[1024,768,1]{1,0,2:T(8,128)S(1)}, u32[]{:S(2)}) copy-start(f32[1024,768,1]{1,0,2:T(8,128)S(1)} %fusion.419) | copy-start | bytes 9437188
  463.7 7.7 copy-start.13
  463.7 7.7 copy-start.222
  486.3 64.7 %copy-start.40 = (bf16[1024,3,48]{0,2,1:T(8,128)(2,1)}, bf16[1024,3,48]{0,2,1:T(8,128)(2,1)S(1)}, u32[]{:S(2)}) copy-start(bf16[1024,3,48]{0,2,1:T(8,128)(2,1)S(1)} %slice.872) | copy-start | bytes 884740
  489.8 7.4 copy-start.82
  497.2 7.4 copy-start.132
  509.8 168.0 %all-reduce.55.cloned.1.call-start = ((), (), s32[]{:S(2)}) async-start(), calls=%async_computation.7 | async-start | bytes 3145728 | tf_op jit(solution)/shard_map/psum | solution.py:217
  510.1 12.0 %slice-start.8 = ((s8[6291456]{0:T(1024)(128)(4,1)}), s8[4194304]{0:T(1024)(128)(4,1)S(1)}, s32[]{:S(2)}) async-start(s8[6291456]{0:T(1024)(128)(4,1)} %bitcast.519), calls=%async_computation.23 | async-start | bytes 8388608
  514.4 7.7 slice-start.9
  528.2 16.1 %copy-start.31 = (f32[1024,768]{1,0:T(8,128)}, f32[1024,768]{1,0:T(8,128)S(1)}, u32[]{:S(2)}) copy-start(f32[1024,768]{1,0:T(8,128)S(1)} %fusion.353) | copy-start | bytes 9437188
  564.3 38.8 %collective-permute-start.2 = (bf16[1024,768]{1,0:T(8,128)(2,1)}, bf16[1024,768]{1,0:T(8,128)(2,1)}, u32[]{:S(2)}, u32[]{:S(2)}) collective-permute-start(bf16[1024,768]{1,0:T(8,128)(2,1)} %get-tuple-element.102), channel_id=1, source_target_pairs={{16,0},{17,1},{18,2},{19,3},{20,4},{21,5},{22,6},{23,7},{24,8},{25... | collective-permute-start | bytes 4718600 | tf_op jit(solution)/shard_map/ppermute | solution.py:17
  578.5 27.8 %copy-start.24 = (bf16[1,192,768]{2,1,0:T(8,128)(2,1)S(1)}, bf16[1,192,768]{2,1,0:T(8,128)(2,1)}, u32[]{:S(2)}) copy-start(bf16[1,192,768]{2,1,0:T(8,128)(2,1)} %copy-done.23) | copy-start | bytes 884740
  578.5 28.5 %copy-start.94 = (bf16[1024,1,192]{0,2,1:T(8,128)(2,1)S(1)}, bf16[1024,1,192]{0,2,1:T(8,128)(2,1)}, u32[]{:S(2)}) copy-start(bf16[1024,1,192]{0,2,1:T(8,128)(2,1)} %slice.867) | copy-start | bytes 1179652
  578.5 28.5 %copy-start.177 = (f32[3,512]{1,0:T(4,128)S(1)}, f32[3,512]{1,0:T(4,128)}, u32[]{:S(2)}) copy-start(f32[3,512]{1,0:T(4,128)} %get-tuple-element.255) | copy-start | bytes 18436
  603.2 11.4 %slice-start.10 = ((s8[6291456]{0:T(1024)(128)(4,1)}), s8[4194304]{0:T(1024)(128)(4,1)S(1)}, s32[]{:S(2)}) async-start(s8[6291456]{0:T(1024)(128)(4,1)} %bitcast.521), calls=%async_computation.25 | async-start | bytes 8388608
  606.3 17.9 %copy-start.6 = (bf16[1024,768]{1,0:T(8,128)(2,1)}, bf16[1024,768]{1,0:T(8,128)(2,1)S(1)}, u32[]{:S(2)}) copy-start(bf16[1024,768]{1,0:T(8,128)(2,1)S(1)} %get-tuple-element.96) | copy-start | bytes 4718596
  607.1 7.5 slice-start.11
  635.0 254.9 %reduce-scatter.13.cloned.1.call-start = ((), (), s32[]{:S(2)}) async-start(), calls=%async_computation.12 | async-start | bytes 491520
  681.9 37.9 %collective-permute-start.3 = (bf16[1024,768]{1,0:T(8,128)(2,1)S(1)}, bf16[1024,768]{1,0:T(8,128)(2,1)S(1)}, u32[]{:S(2)}, u32[]{:S(2)}) collective-permute-start(bf16[1024,768]{1,0:T(8,128)(2,1)S(1)} %get-tuple-element.100), channel_id=1, source_target_pairs={{16,0},{17,1},{18,2},{19,3},{20,4},{21,5},{22,6},{23,7},{24,8},{25... | collective-permute-start | bytes 4718600 | tf_op jit(solution)/shard_map/ppermute | solution.py:17
  691.1 30.8 %slice-start = ((s8[6291456]{0:T(1024)(128)(4,1)}), s8[4194304]{0:T(1024)(128)(4,1)S(1)}, s32[]{:S(2)}) async-start(s8[6291456]{0:T(1024)(128)(4,1)} %bitcast.511), calls=%async_computation.15 | async-start | bytes 8388608
  691.6 30.4 %slice-start.1 = ((s8[6291456]{0:T(1024)(128)(4,1)}), s8[2097152]{0:T(1024)(128)(4,1)S(1)}, s32[]{:S(2)}) async-start(s8[6291456]{0:T(1024)(128)(4,1)} %bitcast.511), calls=%async_computation.16 | async-start | bytes 4194304
  721.2 13.6 %copy-start.9 = (bf16[1024,768]{1,0:T(8,128)(2,1)}, bf16[1024,768]{1,0:T(8,128)(2,1)S(1)}, u32[]{:S(2)}) copy-start(bf16[1024,768]{1,0:T(8,128)(2,1)S(1)} %get-tuple-element.98) | copy-start | bytes 4718596
  736.3 155.3 %all-reduce.57.cloned.1.call-start = ((), (), s32[]{:S(2)}) async-start(), calls=%async_computation.14 | async-start | bytes 6291456 | tf_op jit(solution)/shard_map/psum | solution.py:280
  754.9 143.9 %reduce-scatter.9.cloned.1.call-start = ((), (), s32[]{:S(2)}) async-start(), calls=%async_computation.8 | async-start | bytes 1474560 | tf_op jit(solution)/shard_map/reduce_scatter | solution.py:340
  763.5 137.1 %reduce-scatter.15.cloned.1.call-start = ((), (), s32[]{:S(2)}) async-start(), calls=%async_computation.13 | async-start | bytes 1474560
  777.7 141.1 %reduce-scatter.11.cloned.1.call-start = ((), (), s32[]{:S(2)}) async-start(), calls=%async_computation.9 | async-start | bytes 1474560 | tf_op jit(solution)/shard_map/reduce_scatter | solution.py:349
  778.6 7.2 copy-start.140
  778.6 7.1 copy-start.191
  778.6 7.1 copy-start.232
  796.6 17.0 %copy-start.61 = (bf16[1024,3,64]{0,2,1:T(8,128)(2,1)S(1)}, bf16[1024,3,64]{0,2,1:T(8,128)(2,1)}, u32[]{:S(2)}) copy-start(bf16[1024,3,64]{0,2,1:T(8,128)(2,1)} %copy-done.59) | copy-start | bytes 1179652
  796.6 18.4 %copy-start.168 = (f32[3,192]{1,0:T(4,128)S(1)}, f32[3,192]{1,0:T(4,128)}, u32[]{:S(2)}) copy-start(f32[3,192]{1,0:T(4,128)} %convert_reduce_fusion.14) | copy-start | bytes 6916
  799.7 91.9 %copy-start.12 = (bf16[1024,768]{1,0:T(8,128)(2,1)S(1)}, bf16[1024,768]{1,0:T(8,128)(2,1)}, u32[]{:S(2)}) copy-start(bf16[1024,768]{1,0:T(8,128)(2,1)} %copy-done.9) | copy-start | bytes 4718596
  898.8 21.8 %copy-start.211 = (f32[192]{0:T(256)S(1)}, f32[192]{0:T(256)}, u32[]{:S(2)}) copy-start(f32[192]{0:T(256)} %dynamic-slice_convert_fusion) | copy-start | bytes 2308
  (204 other events, 636.8 us)
Sparse Core Ops, SparseCore 0:
  9.6 39.1 all-gather.10
  50.3 36.6 all-gather.12
  184.9 41.4 all-reduce.48
  312.5 45.5 all-reduce.50
  509.9 45.5 all-reduce.52
  635.2 42.5 all-reduce.54
  736.4 19.9 reduce-scatter.12
  758.9 66.8 all-reduce.56
  828.3 29.4 reduce-scatter.8
  860.1 28.1 reduce-scatter.14
  890.7 27.9 reduce-scatter.10
where the time goes:
time: 937 us; the launch traced here: 928 us
  matrix products  284 us (30%)
  waiting for transfers between devices  240 us (26%)
  blocking collectives  190 us (20%)
  other arithmetic  100 us (11%)
  local copies, waits for them, and re-layouts  80.8 us (9%)
  between operations  19 us (2%)
  starting transfers between devices  13.6 us (1%)
    ppermute x4, waiting for transfers between devices, from_behind(): return lax.ppermute(block, axis, route)  109 us
    sub x12, matrix products, block_softmax(): expont = jnp.exp(scores - row_max)  79.4 us
    psum x3, waiting for transfers between devices, per_device(): lax.psum(partial_sum.astype(jnp.bfloat16), 'tensor').astype(jnp.float32)  75.8 us
    psum x1, blocking collectives, per_device(): norm_sums = lax.psum((grad_gains, grad_shifts), ('fsdp', 'tensor'))  59.7 us
    all_gather x1, blocking collectives, fetch_each(): lax.all_gather(shards[2], 'fsdp', axis=0, tiled=True)  44.2 us
    dot_general x3, matrix products, forward_part(): jnp.dot(active, w_out, preferred_element_type=jnp.float32)  38.2 us
    psum x2, waiting for transfers between devices, backward_local(): lax.psum(grad_rows.astype(jnp.bfloat16), 'tensor').astype(jnp.float32)  38 us
    unnamed x519, local copies, waits for them, and re-layouts  37.2 us
  transfers between devices with their start and end apart: 15, of which 8 were waited for; matrix products, arithmetic and copies ran while one was open for 23% of the time, Pallas kernels for 0%

commit v1 on v0

v1 whole, which is shorter than its diff:
```python
import functools
import math

import jax
import jax.numpy as jnp
from jax import lax
from jax.experimental import pallas as pl
from jax.experimental.pallas import tpu as pltpu
from jax.sharding import PartitionSpec as P

HEAD = 64
PAD = 256
BLOCK = 256
REACH = 512
eps_norm = 1e-05
VMEM_LIMIT = 56 * 1024 * 1024
F32 = jnp.float32
BF16 = jnp.bfloat16


def dot(a, b):
    return jnp.dot(a, b, preferred_element_type=F32)


def dot_t(a, b):
    return lax.dot_general(a, b, (((1,), (1,)), ((), ())), preferred_element_type=F32)


def dot_s(a, b):
    return lax.dot_general(a, b, (((0,), (0,)), ((), ())), preferred_element_type=F32)


def turn(t):
    width = t.shape[-1]
    lane = lax.broadcasted_iota(jnp.int32, t.shape, 1) % HEAD
    return jnp.where(lane < HEAD // 8, -pltpu.roll(t, width - HEAD // 8, 1), pltpu.roll(t, HEAD // 8, 1))


def normed(rows):
    mean = jnp.mean(rows, axis=-1, keepdims=True)
    centred = rows - mean
    var = jnp.mean(centred * centred, axis=-1, keepdims=True)
    inv = lax.rsqrt(var + eps_norm)
    return centred * inv, inv


def tables(cos_ref, sin_ref, rows):
    cos, sin = cos_ref[rows, :], sin_ref[rows, :]
    return jnp.concatenate([cos, cos], axis=1), jnp.concatenate([sin, sin], axis=1)


def head_mask(shape, head):
    lane = lax.broadcasted_iota(jnp.int32, shape, 1)
    return (lane >= head * HEAD) & (lane < (head + 1) * HEAD)


def allowed_keys(segc_ref, segr_ref, low, start, stop):
    shape = (stop - start, stop - low)
    row = start + lax.broadcasted_iota(jnp.int32, shape, 0)
    col = low + lax.broadcasted_iota(jnp.int32, shape, 1)
    return (col <= row) & (segc_ref[start:stop, :] == segr_ref[:, low:stop])


def windows(length):
    return [(max(0, i - REACH), i, i + BLOCK) for i in range(0, length, BLOCK)]


def forward_kernel(
    heads, ff, x_ref, w_ref, vec_ref, bias_ref, cos_ref, sin_ref, segc_ref, segr_ref,
    part_ref, q_ref, k_ref, v_ref, o_ref, lse_ref, m_ref, slope_ref, h1_ref, h2_ref,
):
    length = x_ref.shape[0]
    base = 2 * ff

    @pl.loop(0, length // BLOCK)
    def _(step):
        rows = pl.ds(pl.multiple_of(step * BLOCK, BLOCK), BLOCK)
        xhat, _ = normed(x_ref[rows, :].astype(F32))
        h1 = (xhat * vec_ref[0:1, :] + vec_ref[2:3, :]).astype(BF16)
        h2 = (xhat * vec_ref[1:2, :] + vec_ref[3:4, :]).astype(BF16)
        h1_ref[rows, :] = h1
        h2_ref[rows, :] = h2
        cos, sin = tables(cos_ref, sin_ref, rows)
        q = dot(h1, w_ref[:, base : base + PAD]) + bias_ref[:, ff : ff + PAD]
        k = dot(h1, w_ref[:, base + PAD : base + 2 * PAD]) + bias_ref[:, ff + PAD : ff + 2 * PAD]
        v = dot(h1, w_ref[:, base + 2 * PAD : base + 3 * PAD]) + bias_ref[:, ff + 2 * PAD : ff + 3 * PAD]
        q_ref[rows, :] = ((q * cos + turn(q) * sin) * (1.0 / math.sqrt(HEAD))).astype(BF16)
        k_ref[rows, :] = (k * cos + turn(k) * sin).astype(BF16)
        v_ref[rows, :] = v.astype(BF16)
        a = dot(h2, w_ref[:, 0:ff]) + bias_ref[:, 0:ff]
        cdf = 0.5 * (1.0 + lax.erf(a * (1.0 / math.sqrt(2.0))))
        m = (a * cdf).astype(BF16)
        m_ref[rows, :] = m
        density = jnp.exp(-0.5 * a * a) * (1.0 / math.sqrt(2.0 * math.pi))
        slope_ref[rows, :] = (cdf + a * density).astype(BF16)

    for low, start, stop in windows(length):
        allowed = allowed_keys(segc_ref, segr_ref, low, start, stop)
        q = q_ref[start:stop, :]
        keys, values = k_ref[low:stop, :], v_ref[low:stop, :]
        mix = jnp.zeros((BLOCK, PAD), F32)
        lses = jnp.zeros((BLOCK, 128), F32)
        lane = lax.broadcasted_iota(jnp.int32, (BLOCK, 128), 1)
        for head in range(heads):
            mask = head_mask((BLOCK, PAD), head)
            s = dot_t(jnp.where(mask, q, jnp.zeros_like(q)), keys)
            s = jnp.where(allowed, s, -1000000000.0)
            top = jnp.max(s, axis=-1, keepdims=True)
            e = jnp.exp(s - top)
            total = jnp.sum(e, axis=-1, keepdims=True)
            p = (e * (1.0 / total)).astype(BF16)
            mix = jnp.where(mask, dot(p, values), mix)
            lses = jnp.where(lane == head, top + jnp.log(total), lses)
        o = mix.astype(BF16)
        o_ref[start:stop, :] = o
        lse_ref[start:stop, :] = lses
        part_ref[start:stop, :] = (
            dot_t(o, w_ref[:, base + 3 * PAD : base + 4 * PAD]) + dot_t(m_ref[start:stop, :], w_ref[:, ff : 2 * ff])
        ).astype(BF16)


def backward_kernel(
    heads, ff, x_ref, dy_ref, w_ref, vec_ref, cos_ref, sin_ref, segc_ref, segr_ref,
    q_ref, k_ref, v_ref, lse_ref, slope_ref,
    dx_ref, da_ref, dqkv_ref, sums_ref, bsum_ref,
    dh2_ref, do_ref, dq_ref, dk_ref, dv_ref,
):
    length, width = x_ref.shape
    base = 2 * ff
    sums_ref[...] = jnp.zeros_like(sums_ref)
    bsum_ref[...] = jnp.zeros_like(bsum_ref)
    dk_ref[...] = jnp.zeros_like(dk_ref)
    dv_ref[...] = jnp.zeros_like(dv_ref)

    @pl.loop(0, length // BLOCK)
    def _(step):
        rows = pl.ds(pl.multiple_of(step * BLOCK, BLOCK), BLOCK)
        dy = dy_ref[rows, :]
        do_ref[rows, :] = dot(dy, w_ref[:, base + 3 * PAD : base + 4 * PAD]).astype(BF16)
        da = (dot(dy, w_ref[:, ff : 2 * ff]) * slope_ref[rows, :].astype(F32)).astype(BF16)
        da_ref[rows, :] = da
        bsum_ref[0:1, 0:ff] += jnp.sum(da.astype(F32), axis=0, keepdims=True)
        dh2_ref[rows, :] = dot_t(da, w_ref[:, 0:ff])

    for low, start, stop in windows(length):
        allowed = allowed_keys(segc_ref, segr_ref, low, start, stop)
        q, do = q_ref[start:stop, :], do_ref[start:stop, :]
        keys, values = k_ref[low:stop, :], v_ref[low:stop, :]
        dq = jnp.zeros((BLOCK, PAD), F32)
        for head in range(heads):
            mask = head_mask((BLOCK, PAD), head)
            q_h = jnp.where(mask, q, jnp.zeros_like(q))
            do_h = jnp.where(mask, do, jnp.zeros_like(do))
            s = jnp.where(allowed, dot_t(q_h, keys), -1000000000.0)
            p = jnp.exp(s - lse_ref[start:stop, head : head + 1])
            dp = dot_t(do_h, values)
            ds = (p * (dp - jnp.sum(p * dp, axis=-1, keepdims=True))).astype(BF16)
            dq = jnp.where(mask, dot(ds, keys), dq)
            dk_ref[low:stop, :] += dot_s(ds, q_h)
            dv_ref[low:stop, :] += dot_s(p.astype(BF16), do_h)
        dq_ref[start:stop, :] = dq

    @pl.loop(0, length // BLOCK)
    def _(step):
        rows = pl.ds(pl.multiple_of(step * BLOCK, BLOCK), BLOCK)
        cos, sin = tables(cos_ref, sin_ref, rows)
        dq, dk = dq_ref[rows, :], dk_ref[rows, :]
        dq = (dq * cos - turn(dq) * sin) * (1.0 / math.sqrt(HEAD))
        dk = dk * cos - turn(dk) * sin
        dqkv = jnp.concatenate([dq, dk, dv_ref[rows, :]], axis=1).astype(BF16)
        dqkv_ref[rows, :] = dqkv
        bsum_ref[0:1, ff : ff + 3 * PAD] += jnp.sum(dqkv.astype(F32), axis=0, keepdims=True)
        dh1 = dot_t(dqkv, w_ref[:, base : base + 3 * PAD])
        dh2 = dh2_ref[rows, :]
        xhat, inv = normed(x_ref[rows, :].astype(F32))
        sums_ref[0:1, :] += jnp.sum(dh1 * xhat, axis=0, keepdims=True)
        sums_ref[1:2, :] += jnp.sum(dh2 * xhat, axis=0, keepdims=True)
        sums_ref[2:3, :] += jnp.sum(dh1, axis=0, keepdims=True)
        sums_ref[3:4, :] += jnp.sum(dh2, axis=0, keepdims=True)
        sums_ref[4:5, :] += jnp.sum(dy_ref[rows, :].astype(F32), axis=0, keepdims=True)
        e = dh1 * vec_ref[0:1, :] + dh2 * vec_ref[1:2, :]
        mean_e = jnp.mean(e, axis=-1, keepdims=True)
        mean_ex = jnp.mean(e * xhat, axis=-1, keepdims=True)
        dx_ref[rows, :] = ((e - mean_e - xhat * mean_ex) * inv).astype(BF16)


def weight_kernel(ff, h1_ref, h2_ref, da_ref, dqkv_ref, dy_ref, m_ref, o_ref, g_ref):
    def fill(left_ref, right_ref, offset):
        @pl.loop(0, right_ref.shape[1] // 256)
        def _(step):
            at = pl.multiple_of(step * 256, 256)
            g_ref[:, pl.ds(offset + at, 256)] = dot_s(left_ref[...], right_ref[:, pl.ds(at, 256)]).astype(BF16)

    fill(h2_ref, da_ref, 0)
    fill(dy_ref, m_ref, ff)
    fill(h1_ref, dqkv_ref, 2 * ff)
    fill(dy_ref, o_ref, 2 * ff + 3 * PAD)


def call(kernel, outs, scratch=(), flops=0):
    vm = pl.BlockSpec(memory_space=pltpu.VMEM)

    def run(*args):
        return pl.pallas_call(
            kernel,
            out_shape=[jax.ShapeDtypeStruct(*o) for o in outs],
            in_specs=[vm] * len(args),
            out_specs=[vm] * len(outs),
            scratch_shapes=list(scratch),
            compiler_params=pltpu.CompilerParams(vmem_limit_bytes=VMEM_LIMIT),
            cost_estimate=pl.CostEstimate(flops=flops, bytes_accessed=20_000_000, transcendentals=0),
        )(*args)

    return run


def positions_within(segment):
    positions = jnp.arange(segment.shape[0], dtype=jnp.int32)
    starts = jnp.concatenate([jnp.ones((1,), jnp.bool_), segment[1:] != segment[:-1]])
    first_row = lax.cummax(jnp.where(starts, positions, jnp.zeros_like(positions)), axis=0)
    return (positions - first_row).astype(F32)


def rotary_tables(segment):
    half = HEAD // 8
    freq = 10000.0 ** (-2.0 * jnp.arange(half, dtype=F32) / (HEAD // 4))
    angle = positions_within(segment)[:, None] * freq[None, :]
    cos, sin = jnp.cos(angle), jnp.sin(angle)
    length = segment.shape[0]
    rest = HEAD - 2 * half
    one, zero = jnp.ones((length, rest), F32), jnp.zeros((length, rest), F32)
    return (
        jnp.concatenate([cos, cos, one] * 2, axis=1),
        jnp.concatenate([sin, sin, zero] * 2, axis=1),
    )


def widen(t):
    return jnp.pad(t, [(0, 0)] * (t.ndim - 1) + [(0, PAD - t.shape[-1])])


def per_device(
    tokens, segment_ids, ln_gain, ln_bias, w_qkv, b_qkv, w_o, b_o, w_in, b_in, w_out, b_out, cotangent,
):
    seq_len = segment_ids.shape[1]
    width = tokens.shape[1]
    ff = w_in.shape[2]
    cols = w_o.shape[1]
    heads = cols // HEAD
    piece = w_in.shape[1]
    section = lax.axis_index("section")
    sections = lax.axis_size("section")
    both = ("section", "fsdp")

    small = jnp.concatenate([ln_gain[0], ln_bias[0], b_o, b_out], axis=0).T
    qkv = widen(w_qkv[0]).reshape(piece, 3 * PAD)
    last = jnp.concatenate([w_o[0].T, small, jnp.zeros((piece, PAD - cols - 6), BF16)], axis=1)
    packed = jnp.concatenate([w_in[0], w_out[0].T, qkv, last], axis=1)
    weights = lax.all_gather(packed, both, axis=0, tiled=True).reshape(sections, width, -1)
    biases = jnp.concatenate([b_in, widen(b_qkv[0]).reshape(1, 3 * PAD)], axis=1).astype(F32)
    biases = lax.all_gather(biases, "section", axis=0, tiled=True)
    at = 2 * ff + 3 * PAD + cols
    vectors = jnp.pad(jnp.swapaxes(weights[:, :, at : at + 6], 1, 2).astype(F32), ((0, 0), (0, 2), (0, 0)))

    rows0 = lax.dynamic_slice_in_dim(tokens, section * seq_len, seq_len, 0)
    upstream = lax.dynamic_slice_in_dim(cotangent, section * seq_len, seq_len, 0)
    segment = lax.dynamic_index_in_dim(segment_ids, section, 0, keepdims=False)
    cos, sin = rotary_tables(segment)
    segc, segr = segment[:, None], segment[None, :]

    forward = call(
        functools.partial(forward_kernel, heads, ff),
        [
            ((seq_len, width), BF16), ((seq_len, PAD), BF16), ((seq_len, PAD), BF16), ((seq_len, PAD), BF16),
            ((seq_len, PAD), BF16), ((seq_len, 128), F32), ((seq_len, ff), BF16), ((seq_len, ff), BF16),
            ((seq_len, width), BF16), ((seq_len, width), BF16),
        ],
        flops=5_000_000_000,
    )
    backward = call(
        functools.partial(backward_kernel, heads, ff),
        [
            ((seq_len, width), BF16), ((seq_len, ff), BF16), ((seq_len, 3 * PAD), BF16), ((8, width), F32),
            ((8, ff + 3 * PAD), F32),
        ],
        [
            pltpu.VMEM((seq_len, width), F32), pltpu.VMEM((seq_len, PAD), BF16), pltpu.VMEM((seq_len, PAD), F32),
            pltpu.VMEM((seq_len, PAD), F32), pltpu.VMEM((seq_len, PAD), F32),
        ],
        flops=8_000_000_000,
    )
    weight_grads = call(
        functools.partial(weight_kernel, ff), [((width, 2 * ff + 4 * PAD), BF16)], flops=4_000_000_000
    )

    def run_forward(rows, layer):
        out = forward(rows, weights[layer], vectors[layer], biases[layer][None], cos, sin, segc, segr)
        summed = lax.psum(out[0], "tensor").astype(F32)
        vec = vectors[layer]
        return (rows.astype(F32) + summed + vec[4] + vec[5]).astype(BF16), out[1:]

    def run_backward(rows, dy, layer, saved):
        q, k, v, o, lse, m, slope, h1, h2 = saved
        dx, da, dqkv, sums, bsum = backward(
            rows, dy, weights[layer], vectors[layer], cos, sin, segc, segr, q, k, v, lse, slope
        )
        dx = lax.psum(dx, "tensor").astype(F32)
        (grads,) = weight_grads(h1, h2, da, dqkv, dy, m, o)
        return (dy.astype(F32) + dx).astype(BF16), grads, sums, bsum

    out0, saved0 = run_forward(rows0, 0)
    out1, saved1 = run_forward(out0, 1)
    grad1, gw1, sums1, bsum1 = run_backward(out0, upstream, 1, saved1)
    part1 = lax.psum_scatter(gw1, "fsdp", scatter_dimension=0, tiled=True)
    grad0, gw0, sums0, bsum0 = run_backward(rows0, grad1, 0, saved0)
    part0 = lax.psum_scatter(gw0, "fsdp", scatter_dimension=0, tiled=True)

    down, up = [(1, 0)], [(0, 1)]
    at_first = section == 0

    def exchange(first, second):
        from_one = lax.ppermute(first, "section", down)
        from_zero = lax.ppermute(second, "section", up)
        return jnp.where(at_first, first, second), jnp.where(at_first, from_one, from_zero)

    def whole(first, second):
        own, other = exchange(first, second)
        return jnp.concatenate([jnp.where(at_first, own, other), jnp.where(at_first, other, own)], axis=0)

    outputs = whole(out0, out1)
    input_grads = whole(grad0, grad1)
    own, other = exchange(part0, part1)
    grads = own.astype(F32) + other.astype(F32)

    scale = 1.0 / lax.axis_size("tensor")
    sums = jnp.stack([sums0, sums1])
    sums = jnp.concatenate([sums[:, :4], sums[:, 4:5] * scale], axis=1)
    sums = lax.psum(sums, ("section", "fsdp", "tensor"))
    sums = lax.dynamic_index_in_dim(sums, section, 0, keepdims=False)
    sums = lax.dynamic_slice_in_dim(sums, lax.axis_index("fsdp") * piece, piece, 1)
    bsum = lax.psum(jnp.stack([bsum0[0], bsum1[0]]), both)
    bsum = lax.dynamic_index_in_dim(bsum, section, 0, keepdims=False)
    g_qkv = grads[:, 2 * ff : 2 * ff + 3 * PAD].reshape(piece, 3, PAD)[:, :, :cols]
    return (
        outputs[None],
        input_grads[None],
        sums[0:2][None],
        sums[2:4][None],
        g_qkv[None],
        bsum[ff:].reshape(3, PAD)[:, :cols][None],
        grads[:, 2 * ff + 3 * PAD : 2 * ff + 3 * PAD + cols].T[None],
        sums[4][None],
        grads[:, 0:ff][None],
        bsum[0:ff][None],
        grads[:, ff : 2 * ff].T[None],
        sums[4][None],
    )


def solution(mesh):
    in_specs = (
        P("fsdp", None),
        P("fsdp", None),
        P("section", None, "fsdp"),
        P("section", None, "fsdp"),
        P("section", "fsdp", None, "tensor"),
        P("section", None, "tensor"),
        P("section", "tensor", "fsdp"),
        P("section", "fsdp"),
        P("section", "fsdp", "tensor"),
        P("section", "tensor"),
        P("section", "tensor", "fsdp"),
        P("section", "fsdp"),
        P("fsdp", None),
    )
    out_specs = (
        P("section", "fsdp", None),
        P("section", "fsdp", None),
        P("section", None, "fsdp"),
        P("section", None, "fsdp"),
        P("section", "fsdp", None, "tensor"),
        P("section", None, "tensor"),
        P("section", "tensor", "fsdp"),
        P("section", "fsdp"),
        P("section", "fsdp", "tensor"),
        P("section", "tensor"),
        P("section", "tensor", "fsdp"),
        P("section", "fsdp"),
    )
    return jax.shard_map(
        per_device, mesh=mesh, in_specs=in_specs, out_specs=out_specs, check_vma=False
    )
```

time: 937 us -> 568 us (0.61)
  matrix products: 284 us -> 0 us
  Pallas kernels: 0 us -> 100 us
  blocking collectives: 190 us -> 98.6 us
  other arithmetic: 100 us -> 27.2 us
  local copies, waits for them, and re-layouts: 80.8 us -> 31.1 us
  waiting for transfers between devices: 240 us -> 271 us
    dot_general x69 -> x0, matrix products: 195 us -> none  [the longest x3 38.2 us: forward_part(): jnp.dot(active, w_out, preferred_element_type=jnp.float32)]
    all_gather x2 -> x1, waiting for transfers between devices: 0.01 us -> 105 us  [per_device(): lax.all_gather(packed, both, axis=0, tiled=True)]
    pallas_call x0 -> x6, Pallas kernels: none -> 100 us  [run(): pl.pallas_call(kernel, out_shape=[jax.ShapeDtypeStruct(*o) for o in outs]...]
    all_gather x4 -> x1, blocking collectives: 99.9 us -> 5.54 us  [per_device(): biases = lax.all_gather(biases, 'section', axis=0, tiled=True)]
    ppermute x4 -> x6, waiting for transfers between devices: 109 us -> 16.7 us  [the longest x3 16.7 us: exchange(): from_one = lax.ppermute(first, 'section', down)]
    sub x12 -> x0, matrix products: 79.4 us -> none  [block_softmax(): expont = jnp.exp(scores - row_max)]
    unnamed x519 -> x47, local copies, waits for them, and re-layouts: 37.2 us -> 5.38 us
    dynamic_update_slice x9 -> x0, other arithmetic: 25.7 us -> none  [the longest x3 11.6 us: per_device(): lax.dynamic_update_slice_in_dim(input_grads, jnp.where(is_live, grad_b, c...]
  transfers between devices with their start and end apart: 15 -> 12, of which waited for: 8 -> 6; matrix products, arithmetic and copies ran while one was open for 23% -> 6% of each run, Pallas kernels for 0% -> 4%
where the time goes in v1:
time: 568 us; the launch traced here: 563 us
  waiting for transfers between devices  271 us (48%)
  Pallas kernels  100 us (18%)
  blocking collectives  98.6 us (17%)
  local copies, waits for them, and re-layouts  31.1 us (5%)
  other arithmetic  27.2 us (5%)
  starting transfers between devices  21 us (4%)
  between operations  14.8 us (3%)
    all_gather x1, waiting for transfers between devices, per_device(): lax.all_gather(packed, both, axis=0, tiled=True)  105 us
    pallas_call x6, Pallas kernels, run(): pl.pallas_call(kernel, out_shape=[jax.ShapeDtypeStruct(*o) for o in outs]...  100 us
    psum x2, waiting for transfers between devices, run_forward(): summed = lax.psum(out[0], 'tensor').astype(F32)  76 us
    psum x1, blocking collectives, per_device(): sums = lax.psum(sums, ('section', 'fsdp', 'tensor'))  56.1 us
    psum x1, waiting for transfers between devices, run_backward(): dx = lax.psum(dx, 'tensor').astype(F32)  43 us
    psum x1, blocking collectives, per_device(): bsum = lax.psum(jnp.stack([bsum0[0], bsum1[0]]), both)  37 us
    reduce_scatter x1, waiting for transfers between devices, per_device(): part0 = lax.psum_scatter(gw0, 'fsdp', scatter_dimension=0, tiled=True)  30.1 us
    ppermute x3, waiting for transfers between devices, exchange(): from_one = lax.ppermute(first, 'section', down)  16.7 us
  transfers between devices with their start and end apart: 12, of which 6 were waited for; matrix products, arithmetic and copies ran while one was open for 6% of the time, Pallas kernels for 4%

profile of v1, /device:TPU:0, one launch (start us, length us, event | category | flops | bytes accessed | tf_op | source)
XLA Modules:
  0.0 563.4 jit_solution(14824202019319020517)
XLA Ops:
  7.3 1.3 copy.68
  8.6 0.2 pad.12.clone
  8.9 0.1 copy.57
  9.0 0.1 copy.58
  9.2 1.1 concatenate.40
  10.5 0.1 compare_reduce_fusion
  10.6 0.3 reduce-window.9
  11.0 1.0 copy.61.segc_ref
  12.1 0.1 slice_reduce_fusion
  12.3 1.9 multiply_sine_fusion
  14.2 1.7 concatenate.45.cos_ref
  16.0 1.7 concatenate.46.sin_ref
  17.8 5.5 all-gather
  23.4 0.6 constant_dynamic-slice_fusion.3.segr_ref
  24.0 2.7 constant_dynamic-slice_fusion.4.x_ref
  26.6 0.6 slice_bitcast_fusion.4
  27.2 104.7 %all-gather.3.cloned.1.call-done = bf16[1536,2560]{1,0:T(8,128)(2,1)} async-done(((bf16[192,2560]{1,0:T(8,128)(2,1)}), bf16[1536,2560]{1,0:T(8,128)(2,1)}) %all-gather.3.cloned.1.call-update) | async-done | bytes 7864336 | tf_op jit(solution)/shard_map/all_gather | solution.py:259
  131.9 1.2 slice.155
  133.1 0.2 copy.67
  133.3 0.6 fusion.1
  133.9 5.7 %fusion.6 = (bf16[768,2560]{1,0:T(8,128)(2,1)}, bf16[768,2560]{1,0:T(8,128)(2,1)}) fusion(bf16[1536,2560]{1,0:T(8,128)(2,1)} %all-gather.3.cloned.1.call-done), kind=kLoop, calls=%fused_computation.57 | loop fusion | bytes 15728640 | tf_op jit(solution)/shard_map/slice | solution.py:297
  139.5 15.6 %shard_map.220 = (bf16[1024,768]{1,0:T(8,128)(2,1)}, bf16[1024,256]{1,0:T(8,128)(2,1)}, bf16[1024,256]{1,0:T(8,128)(2,1)}, bf16[1024,256]{1,0:T(8,128)(2,1)}, bf...) custom-call(bf16[1024,768]{1,0:T(8,128)(2,1)} %constant_dynamic-slic, ...), custom_call_target="tpu_custom_call" | custom-call | flops 5000000000 | bytes 20000000 | tf_op jit(solution)/shard_map/pallas_call | solution.py:204
  155.2 0.6 all-reduce.10.cloned.1.call-start
  155.8 3.0 constant_dynamic-slice_fusion.2.dy_ref
  158.8 37.6 %all-reduce.8.cloned.1.call-done = bf16[1024,768]{1,0:T(8,128)(2,1)} async-done(((bf16[1024,768]{1,0:T(8,128)(2,1)}), bf16[1024,768]{1,0:T(8,128)(2,1)}) %all-reduce.8.cloned.1.call-update) | async-done | bytes 1572880 | tf_op jit(solution)/shard_map/psum | solution.py:298
  196.4 3.1 add_convert_fusion.3.x_ref
  199.5 15.6 %shard_map.221 = (bf16[1024,768]{1,0:T(8,128)(2,1)}, bf16[1024,256]{1,0:T(8,128)(2,1)}, bf16[1024,256]{1,0:T(8,128)(2,1)}, bf16[1024,256]{1,0:T(8,128)(2,1)}, bf...) custom-call(bf16[1024,768]{1,0:T(8,128)(2,1)} %add_convert_fusion.3., ...), custom_call_target="tpu_custom_call" | custom-call | flops 5000000000 | bytes 20000000 | tf_op jit(solution)/shard_map/pallas_call | solution.py:204
  215.2 22.3 %shard_map.222 = (bf16[1024,768]{1,0:T(8,128)(2,1)}, bf16[1024,768]{1,0:T(8,128)(2,1)}, bf16[1024,768]{1,0:T(8,128)(2,1)}, f32[8,768]{1,0:T(8,128)}, f32[8,1536]{1,0:T(8,128)}) custom-call(bf16[1024,768]{1,0:T(8,128)(2,1)} %add_convert_fusion.3.x_ref, bf16[1024,768]{1,0:T(8,128)(2,1)} %constant_dynamic-slice_fusion.2.dy_ref, ...), custom_call_target="tpu_custom_call" | custom-call | flops 8000000000 | bytes 20000000 | tf_op jit(solution)/shard_map/pallas_call | solution.py:204
  237.6 43.0 %all-reduce.10.cloned.1.call-done = bf16[1024,768]{1,0:T(8,128)(2,1)} async-done(((bf16[1024,768]{1,0:T(8,128)(2,1)}), bf16[1024,768]{1,0:T(8,128)(2,1)}) %all-reduce.10.cloned.1.call-update) | async-done | bytes 1572880 | tf_op jit(solution)/shard_map/psum | solution.py:307
  280.6 3.0 add_convert_fusion.1.dy_ref
  283.6 22.2 %shard_map.223 = (bf16[1024,768]{1,0:T(8,128)(2,1)}, bf16[1024,768]{1,0:T(8,128)(2,1)}, bf16[1024,768]{1,0:T(8,128)(2,1)}, f32[8,768]{1,0:T(8,128)}, f32[8,1536]{1,0:T(8,128)}) custom-call(bf16[1024,768]{1,0:T(8,128)(2,1)} %constant_dynamic-slice_fusion.4.x_ref, bf16[1024,768]{1,0:T(8,128)(2,1)} %add_convert_fusion.1.dy_ref, ...), custom_call_target="tpu_custom_call" | custom-call | flops 8000000000 | bytes 20000000 | tf_op jit(solution)/shard_map/pallas_call | solution.py:204
  305.9 12.0 %shard_map.225 = bf16[768,2560]{1,0:T(8,128)(2,1)} custom-call(bf16[1024,768]{1,0:T(8,128)(2,1)} %get-tuple-element.64.h1_ref, bf16[1024,768]{1,0:T(8,128)(2,1)} %get-tuple-element.65.h2_ref, bf16[1024,768]{1,0:T(8,128)(2,1)} %get-tuple-element.66.da_ref, bf16[1024,768]{1,0:T(8,128)(2,1)} %get-tuple-element.67.dqkv_ref, ...), custom_call_target="tpu_custom_call" | custom-call | flops 4000000000 | bytes 20000000 | tf_op jit(solution)/shard_map/pallas_call | solution.py:204
  318.0 12.3 %shard_map.224 = bf16[768,2560]{1,0:T(8,128)(2,1)} custom-call(bf16[1024,768]{1,0:T(8,128)(2,1)} %get-tuple-element.58.h1_ref, bf16[1024,768]{1,0:T(8,128)(2,1)} %get-tuple-element.59.h2_ref, bf16[1024,768]{1,0:T(8,128)(2,1)} %get-tuple-element.60.da_ref, bf16[1024,768]{1,0:T(8,128)(2,1)} %get-tuple-element.61.dqkv_ref, ...), custom_call_target="tpu_custom_call" | custom-call | flops 4000000000 | bytes 20000000 | tf_op jit(solution)/shard_map/pallas_call | solution.py:204
  330.3 1.4 copy-done.1
  331.7 4.6 collective-permute-start.3
  336.2 38.4 %all-reduce.12.cloned.1.call-done = (bf16[1024,768]{1,0:T(8,128)(2,1)}, bf16[1024,768]{1,0:T(8,128)(2,1)}) async-done(((bf16[1024,768]{1,0:T(8,128)(2,1)}, bf16[1024,768]{1,0:T(8,128)(2,1)}), (bf16[1024,768]{1,0:T(8,128)(2,1)}, bf16[1024,768]{1,0:T(8,128)(2,1)})) %all-reduce.12.cloned.1.call-update) | async-done | bytes 3145744 | tf_op jit(solution)/shard_map/psum | solution.py:298
  374.7 3.1 add_convert_fusion
  377.7 1.3 collective-permute-start.2
  379.0 1.3 collective-permute-start
  380.3 0.8 slice.143
  381.1 0.8 slice.142
  381.9 3.6 add_convert_fusion.2
  385.5 7.6 %collective-permute-start.1 = (bf16[1024,768]{1,0:T(8,128)(2,1)}, bf16[1024,768]{1,0:T(8,128)(2,1)}, u32[]{:S(2)}, u32[]{:S(2)}) collective-permute-start(bf16[1024,768]{1,0:T(8,128)(2,1)} %add_convert_fusion.2), channel_id=1, source_target_pairs={{0,16},{1,17},{2,18},{3,19},{4,20},{5,21},{6,22},{7,23},{8,24},{9,... | collective-permute-start | bytes 4718600 | tf_op jit(solution)/shard_map/ppermute | solution.py:323
  393.1 37.0 %psum.47 = f32[2,1536]{1,0:T(2,128)S(1)} all-reduce(f32[2,1536]{1,0:T(2,128)S(1)} %pad_maximum_fusion.1), channel_id=1, replica_groups=mesh['section'=2,'fsdp'=4,'tensor'=4] {'section','fsdp'}, use_global_device_ids=true, to_apply=%region_9.10 | all-reduce | flops 3072 | bytes 24576 | tf_op jit(solution)/shard_map/psum | solution.py:341
  430.1 0.6 constant_dynamic-slice_fusion.1
  430.7 0.6 broadcast_in_dim.50
  431.4 56.1 %psum.46 = f32[2,5,768]{2,1,0:T(8,128)S(1)} all-reduce(f32[2,5,768]{2,1,0:T(8,128)S(1)} %pad_maximum_fusion), channel_id=1, replica_groups=mesh['section'=2,'fsdp'=4,'tensor'=4] {'section','fsdp','tensor'}, use_global_device_ids=true, to_apply=%region_6.7 | all-reduce | flops 7680 | bytes 61440 | tf_op jit(solution)/shard_map/psum | solution.py:338
  487.4 0.1 dynamic-slice_bitcast_fusion
  487.5 0.7 fusion.7
  488.2 4.1 broadcast_select_fusion.1
  492.3 4.2 collective-permute-start.5
  496.5 30.1 %reduce-scatter.3.cloned.1.call-done = bf16[192,2560]{1,0:T(8,128)(2,1)} async-done(((bf16[768,2560]{1,0:T(8,128)(2,1)}), bf16[192,2560]{1,0:T(8,128)(2,1)}) %reduce-scatter.3.cloned.1.call-update) | async-done | bytes 983056 | tf_op jit(solution)/shard_map/reduce_scatter | solution.py:316
  526.5 1.3 collective-permute-start.4
  527.8 3.7 maximum_bitcast_fusion.1
  531.6 1.8 broadcast_select_fusion.5
  533.4 1.9 maximum_bitcast_fusion
  535.2 16.7 %collective-permute-done.4 = bf16[192,2560]{1,0:T(8,128)(2,1)S(1)} collective-permute-done((bf16[192,2560]{1,0:T(8,128)(2,1)}, bf16[192,2560]{1,0:T(8,128)(2,1)S(1)}, u32[]{:S(2)}, u32[]{:S(2)}) %collective-permute-start.4) | collective-permute-done | bytes 983072 | tf_op jit(solution)/shard_map/ppermute | solution.py:322
  552.0 0.4 convert_add_fusion
  552.4 1.1 slice_bitcast_fusion.1
  553.6 0.3 reshape.132
  553.9 0.1 slice_bitcast_fusion
  554.0 0.9 copy.65
  555.0 0.8 copy.66
  555.8 0.6 copy.76
  (76 shorter events, 1.0 us)
Async XLA Ops:
  7.2 1.7 copy-start.8
  7.2 1.8 copy-start.18
  7.2 1.8 copy-start.17
  7.2 1.8 copy-start.16
  7.2 1.8 copy-start.15
  7.2 2.0 copy-start.6
  7.2 2.0 copy-start.7
  7.3 124.6 %all-gather.3.cloned.1.call-start = ((), (), s32[]{:S(2)}) async-start(), calls=%async_computation.2 | async-start | bytes 8847360 | tf_op jit(solution)/shard_map/all_gather | solution.py:259
  9.2 1.3 copy-start.11
  9.2 2.9 copy-start.14
  10.4 186.0 %all-reduce.8.cloned.1.call-start = ((), (), s32[]{:S(2)}) async-start(), calls=%async_computation.3 | async-start | bytes 3145728 | tf_op jit(solution)/shard_map/psum | solution.py:298
  16.0 1.8 copy-start.13
  155.2 41.2 %copy-start.2 = (bf16[2048,768]{1,0:T(8,128)(2,1)S(1)}, bf16[2048,768]{1,0:T(8,128)(2,1)}, u32[]{:S(2)}) copy-start(bf16[2048,768]{1,0:T(8,128)(2,1)} %param.13) | copy-start | bytes 9437188
  155.2 125.4 %all-reduce.10.cloned.1.call-start = ((), (), s32[]{:S(2)}) async-start(), calls=%async_computation.4 | async-start | bytes 3145728 | tf_op jit(solution)/shard_map/psum | solution.py:307
  215.2 65.4 %copy-start.3 = (bf16[2048,768]{1,0:T(8,128)(2,1)S(1)}, bf16[2048,768]{1,0:T(8,128)(2,1)}, u32[]{:S(2)}) copy-start(bf16[2048,768]{1,0:T(8,128)(2,1)} %param.25) | copy-start | bytes 9437188
  237.5 137.1 %all-reduce.12.cloned.1.call-start = ((), (), s32[]{:S(2)}) async-start(), calls=%async_computation.7 | async-start | bytes 6291456 | tf_op jit(solution)/shard_map/psum | solution.py:298
  305.8 186.5 %reduce-scatter.5.cloned.1.call-start = ((), (), s32[]{:S(2)}) async-start(), calls=%async_computation.6 | async-start | bytes 4915200 | tf_op jit(solution)/shard_map/reduce_scatter | solution.py:314
  317.9 208.6 %reduce-scatter.3.cloned.1.call-start = ((), (), s32[]{:S(2)}) async-start(), calls=%async_computation.5 | async-start | bytes 4915200 | tf_op jit(solution)/shard_map/reduce_scatter | solution.py:316
  330.2 1.4 copy-start.1
  331.7 156.5 %collective-permute-start.3 = (bf16[1024,768]{1,0:T(8,128)(2,1)S(1)}, bf16[1024,768]{1,0:T(8,128)(2,1)}, u32[]{:S(2)}, u32[]{:S(2)}) collective-permute-start(bf16[1024,768]{1,0:T(8,128)(2,1)S(1)} %copy-done.1), channel_id=1, source_target_pairs={{0,16},{1,17},{2,18},{3,19},{4,20},{5,21},{6,22},{7,23},{8,24},{9,... | collective-permute-start | bytes 4718600 | tf_op jit(solution)/shard_map/ppermute | solution.py:323
  374.7 4.4 copy-start
  377.7 110.5 %collective-permute-start.2 = (bf16[1024,768]{1,0:T(8,128)(2,1)}, bf16[1024,768]{1,0:T(8,128)(2,1)}, u32[]{:S(2)}, u32[]{:S(2)}) collective-permute-start(bf16[1024,768]{1,0:T(8,128)(2,1)} %add_convert_fusion), channel_id=1, source_target_pairs={{16,0},{17,1},{18,2},{19,3},{20,4},{21,5},{22,6},{23,7},{24,8},{25... | collective-permute-start | bytes 4718600 | tf_op jit(solution)/shard_map/ppermute | solution.py:322
  379.0 152.6 %collective-permute-start = (bf16[1024,768]{1,0:T(8,128)(2,1)S(1)}, bf16[1024,768]{1,0:T(8,128)(2,1)}, u32[]{:S(2)}, u32[]{:S(2)}) collective-permute-start(bf16[1024,768]{1,0:T(8,128)(2,1)S(1)} %copy-done), channel_id=1, source_target_pairs={{16,0},{17,1},{18,2},{19,3},{20,4},{21,5},{22,6},{23,7},{24,8},{25... | collective-permute-start | bytes 4718600 | tf_op jit(solution)/shard_map/ppermute | solution.py:322
  381.9 49.4 %copy-start.9 = (f32[8,768]{1,0:T(8,128)S(1)}, f32[8,768]{1,0:T(8,128)}, u32[]{:S(2)}) copy-start(f32[8,768]{1,0:T(8,128)} %get-tuple-element.57) | copy-start | bytes 73732
  381.9 49.4 %copy-start.10 = (f32[8,768]{1,0:T(8,128)S(1)}, f32[8,768]{1,0:T(8,128)}, u32[]{:S(2)}) copy-start(f32[8,768]{1,0:T(8,128)} %get-tuple-element.56) | copy-start | bytes 73732
  385.5 146.1 %collective-permute-start.1 = (bf16[1024,768]{1,0:T(8,128)(2,1)}, bf16[1024,768]{1,0:T(8,128)(2,1)}, u32[]{:S(2)}, u32[]{:S(2)}) collective-permute-start(bf16[1024,768]{1,0:T(8,128)(2,1)} %add_convert_fusion.2), channel_id=1, source_target_pairs={{0,16},{1,17},{2,18},{3,19},{4,20},{5,21},{6,22},{7,23},{8,24},{9,... | collective-permute-start | bytes 4718600 | tf_op jit(solution)/shard_map/ppermute | solution.py:323
  487.5 68.2 %copy-start.12 = (f32[1,192]{1,0:T(1,128)}, f32[1,192]{1,0:T(1,128)S(1)}, u32[]{:S(2)}) copy-start(f32[1,192]{1,0:T(1,128)S(1)} %dynamic-slice_bitcast_fusion) | copy-start | bytes 2308
  492.3 43.0 %collective-permute-start.5 = (bf16[192,2560]{1,0:T(8,128)(2,1)}, bf16[192,2560]{1,0:T(8,128)(2,1)S(1)}, u32[]{:S(2)}, u32[]{:S(2)}) collective-permute-start(bf16[192,2560]{1,0:T(8,128)(2,1)} %reduce-scatter.5.cloned.1.call-done), channel_id=1, source_target_pairs={{0,16},{1,17},{2,18},{3,19},{4,20},{5,21},{6,22},{7,23},{8,24},{9,... | collective-permute-start | bytes 2949128 | tf_op jit(solution)/shard_map/ppermute | solution.py:323
  526.5 25.4 %collective-permute-start.4 = (bf16[192,2560]{1,0:T(8,128)(2,1)}, bf16[192,2560]{1,0:T(8,128)(2,1)S(1)}, u32[]{:S(2)}, u32[]{:S(2)}) collective-permute-start(bf16[192,2560]{1,0:T(8,128)(2,1)} %reduce-scatter.3.cloned.1.call-done), channel_id=1, source_target_pairs={{16,0},{17,1},{18,2},{19,3},{20,4},{21,5},{22,6},{23,7},{24,8},{25... | collective-permute-start | bytes 2949128 | tf_op jit(solution)/shard_map/ppermute | solution.py:322
  533.4 18.6 %copy-start.4 = (bf16[192,2560]{1,0:T(8,128)(2,1)S(1)}, bf16[192,2560]{1,0:T(8,128)(2,1)}, u32[]{:S(2)}) copy-start(bf16[192,2560]{1,0:T(8,128)(2,1)} %reduce-scatter.5.cloned.1.call-done) | copy-start | bytes 2949124
  533.4 18.6 %copy-start.5 = (bf16[192,2560]{1,0:T(8,128)(2,1)S(1)}, bf16[192,2560]{1,0:T(8,128)(2,1)}, u32[]{:S(2)}) copy-start(bf16[192,2560]{1,0:T(8,128)(2,1)} %reduce-scatter.3.cloned.1.call-done) | copy-start | bytes 2949124
Sparse Core Ops, SparseCore 0:
  10.8 121.0 all-gather.2
  155.3 41.0 all-reduce.7
  237.6 42.9 all-reduce.9
  305.9 68.6 all-reduce.11
  376.8 73.8 reduce-scatter.4
  452.8 73.6 reduce-scatter.2

commit v2 on v1

--- a/solution.py
+++ b/solution.py
@@ -235,6 +235,26 @@
     )
 
 
+def tensor_sum(part):
+    devices = range(lax.axis_size("tensor"))
+    index = lax.axis_index("tensor")
+
+    def halves(block, bit):
+        size = block.shape[0] // 2
+        place = (index // bit) % 2
+        keep = lax.dynamic_slice_in_dim(block, place * size, size, 0)
+        send = lax.dynamic_slice_in_dim(block, (1 - place) * size, size, 0)
+        got = lax.ppermute(send, "tensor", [(i, i ^ bit) for i in devices])
+        return (keep.astype(F32) + got.astype(F32)).astype(BF16)
+
+    def join(block, bit):
+        first = (index // bit) % 2 == 0
+        got = lax.ppermute(block, "tensor", [(i, i ^ bit) for i in devices])
+        return jnp.concatenate([jnp.where(first, block, got), jnp.where(first, got, block)], axis=0)
+
+    return join(join(halves(halves(part, 1), 2), 2), 1)
+
+
 def widen(t):
     return jnp.pad(t, [(0, 0)] * (t.ndim - 1) + [(0, PAD - t.shape[-1])])
 
@@ -295,7 +315,7 @@
 
     def run_forward(rows, layer):
         out = forward(rows, weights[layer], vectors[layer], biases[layer][None], cos, sin, segc, segr)
-        summed = lax.psum(out[0], "tensor").astype(F32)
+        summed = (lax.psum(out[0], "tensor") if layer == 0 else tensor_sum(out[0])).astype(F32)
         vec = vectors[layer]
         return (rows.astype(F32) + summed + vec[4] + vec[5]).astype(BF16), out[1:]
 
@@ -304,8 +324,10 @@
         dx, da, dqkv, sums, bsum = backward(
             rows, dy, weights[layer], vectors[layer], cos, sin, segc, segr, q, k, v, lse, slope
         )
-        dx = lax.psum(dx, "tensor").astype(F32)
+        dx = tensor_sum(dx)
         (grads,) = weight_grads(h1, h2, da, dqkv, dy, m, o)
+        dx, grads = lax.optimization_barrier((dx, grads))
+        dx = dx.astype(F32)
         return (dy.astype(F32) + dx).astype(BF16), grads, sums, bsum
 
     out0, saved0 = run_forward(rows0, 0)

time: 568 us -> 523 us (0.921)
  waiting for transfers between devices: 271 us -> 216 us
  other arithmetic: 27.2 us -> 33.3 us
    psum x3 -> x1, waiting for transfers between devices: 119 us -> 37.7 us  [run_forward(): lax.psum(out[0], 'tensor')]
    ppermute x0 -> x12, waiting for transfers between devices: none -> 56.9 us  [the longest x6 32 us: halves(): got = lax.ppermute(send, 'tensor', [(i, i ^ bit) for i in devices])]
    reduce_scatter x1, waiting for transfers between devices: 30.1 us -> 0.02 us  [per_device(): part0 = lax.psum_scatter(gw0, 'fsdp', scatter_dimension=0, tiled=True)]
    ppermute x3, waiting for transfers between devices: 16.7 us -> 4.1 us  [exchange(): from_one = lax.ppermute(first, 'section', down)]
    ppermute x3, waiting for transfers between devices: 0.01 us -> 12.1 us  [exchange(): from_zero = lax.ppermute(second, 'section', up)]
  transfers between devices with their start and end apart: 12 -> 22, of which waited for: 6 -> 12; matrix products, arithmetic and copies ran while one was open for 6% -> 9% of each run, Pallas kernels for 4% -> 9%
where the time goes in v2:
time: 523 us; the launch traced here: 518 us
  waiting for transfers between devices  216 us (41%)
  Pallas kernels  100 us (19%)
  blocking collectives  95 us (18%)
  local copies, waits for them, and re-layouts  34.6 us (7%)
  other arithmetic  33.3 us (6%)
  starting transfers between devices  24.7 us (5%)
  between operations  14.9 us (3%)
    all_gather x1, waiting for transfers between devices, per_device(): lax.all_gather(packed, both, axis=0, tiled=True)  105 us
    pallas_call x6, Pallas kernels, run(): pl.pallas_call(kernel, out_shape=[jax.ShapeDtypeStruct(*o) for o in outs]...  100 us
    psum x1, blocking collectives, per_device(): sums = lax.psum(sums, ('section', 'fsdp', 'tensor'))  51.5 us
    psum x1, blocking collectives, per_device(): bsum = lax.psum(jnp.stack([bsum0[0], bsum1[0]]), both)  38 us
    psum x1, waiting for transfers between devices, run_forward(): lax.psum(out[0], 'tensor')  37.7 us
    ppermute x6, waiting for transfers between devices, halves(): got = lax.ppermute(send, 'tensor', [(i, i ^ bit) for i in devices])  32 us
    ppermute x6, waiting for transfers between devices, join(): got = lax.ppermute(block, 'tensor', [(i, i ^ bit) for i in devices])  25 us
    ppermute x3, starting transfers between devices, exchange(): from_zero = lax.ppermute(second, 'section', up)  16.8 us
  transfers between devices with their start and end apart: 22, of which 12 were waited for; matrix products, arithmetic and copies ran while one was open for 9% of the time, Pallas kernels for 9%

profile of v2, /device:TPU:0, one launch (start us, length us, event | category | flops | bytes accessed | tf_op | source)
XLA Modules:
  0.0 518.5 jit_solution(2707005731925769111)
XLA Ops:
  7.3 1.3 copy.68
  9.2 1.1 concatenate.58
  11.0 1.0 copy.61.segc_ref
  12.3 1.9 multiply_sine_fusion
  14.2 1.7 concatenate.63.cos_ref
  16.0 1.7 concatenate.64.sin_ref
  17.8 5.5 %all-gather = f32[2,1,1536]{2,1,0:T(1,128)S(1)} all-gather(f32[1,1,1536]{2,1,0:T(1,128)S(1)} %fusion.4), channel_id=1, replica_groups=mesh['section'=2,'fsdp'=4,'tensor'=4] {'section'}, dimensions={0}, use_global_device_ids=true | all-gather | bytes 18432 | tf_op jit(solution)/shard_map/all_gather | solution.py:281
  23.4 0.6 constant_dynamic-slice_fusion.10.segr_ref
  23.9 2.7 constant_dynamic-slice_fusion.11.x_ref
  26.6 0.6 slice_bitcast_fusion.4
  27.2 104.7 %all-gather.3.cloned.1.call-done = bf16[1536,2560]{1,0:T(8,128)(2,1)} async-done(((bf16[192,2560]{1,0:T(8,128)(2,1)}), bf16[1536,2560]{1,0:T(8,128)(2,1)}) %all-gather.3.cloned.1.call-update) | async-done | bytes 7864336 | tf_op jit(solution)/shard_map/all_gather | solution.py:279
  131.9 1.2 slice.155
  133.3 0.6 fusion.1
  133.9 5.5 %fusion.6 = (bf16[768,2560]{1,0:T(8,128)(2,1)}, bf16[768,2560]{1,0:T(8,128)(2,1)}) fusion(bf16[1536,2560]{1,0:T(8,128)(2,1)} %all-gather.3.cloned.1.call-done), kind=kLoop, calls=%fused_computation.87 | loop fusion | bytes 15728640 | tf_op jit(solution)/shard_map/slice | solution.py:317
  139.4 15.6 %shard_map.220 = (bf16[1024,768]{1,0:T(8,128)(2,1)}, bf16[1024,256]{1,0:T(8,128)(2,1)}, bf16[1024,256]{1,0:T(8,128)(2,1)}, bf16[1024,256]{1,0:T(8,128)(2,1)}, bf...) custom-call(bf16[1024,768]{1,0:T(8,128)(2,1)} %constant_dynamic-slic, ...), custom_call_target="tpu_custom_call" | custom-call | flops 5000000000 | bytes 20000000 | tf_op jit(solution)/shard_map/pallas_call | solution.py:204
  155.7 2.8 constant_dynamic-slice_fusion.7.dy_ref
  158.6 37.7 %all-reduce.5.cloned.1.call-done = bf16[1024,768]{1,0:T(8,128)(2,1)} async-done(((bf16[1024,768]{1,0:T(8,128)(2,1)}), bf16[1024,768]{1,0:T(8,128)(2,1)}) %all-reduce.5.cloned.1.call-update) | async-done | bytes 1572880 | tf_op jit(solution)/shard_map/psum | solution.py:318
  196.3 3.1 add_convert_fusion.3.x_ref
  199.4 15.7 %shard_map.221 = (bf16[1024,768]{1,0:T(8,128)(2,1)}, bf16[1024,256]{1,0:T(8,128)(2,1)}, bf16[1024,256]{1,0:T(8,128)(2,1)}, bf16[1024,256]{1,0:T(8,128)(2,1)}, bf...) custom-call(bf16[1024,768]{1,0:T(8,128)(2,1)} %add_convert_fusion.3., ...), custom_call_target="tpu_custom_call" | custom-call | flops 5000000000 | bytes 20000000 | tf_op jit(solution)/shard_map/pallas_call | solution.py:204
  215.1 22.2 %shard_map.222 = (bf16[1024,768]{1,0:T(8,128)(2,1)}, bf16[1024,768]{1,0:T(8,128)(2,1)}, bf16[1024,768]{1,0:T(8,128)(2,1)}, f32[8,768]{1,0:T(8,128)}, f32[8,1536]{1,0:T(8,128)}) custom-call(bf16[1024,768]{1,0:T(8,128)(2,1)} %add_convert_fusion.3.x_ref, bf16[1024,768]{1,0:T(8,128)(2,1)} %constant_dynamic-slice_fusion.7.dy_ref, ...), custom_call_target="tpu_custom_call" | custom-call | flops 8000000000 | bytes 20000000 | tf_op jit(solution)/shard_map/pallas_call | solution.py:204
  237.3 1.3 constant_dynamic-slice_fusion.6
  238.8 2.2 collective-permute-done.6
  241.6 10.8 %collective-permute-done.7 = bf16[256,768]{1,0:T(8,128)(2,1)S(1)} collective-permute-done((bf16[256,768]{1,0:T(8,128)(2,1)S(1)}, bf16[256,768]{1,0:T(8,128)(2,1)S(1)}, u32[]{:S(2)}, u32[]{:S(2)}) %collective-permute-start.7) | collective-permute-done | bytes 393248 | tf_op jit(solution)/shard_map/ppermute | solution.py:247
  252.9 10.0 %collective-permute-done.8 = bf16[256,768]{1,0:T(8,128)(2,1)S(1)} collective-permute-done((bf16[256,768]{1,0:T(8,128)(2,1)S(1)}, bf16[256,768]{1,0:T(8,128)(2,1)S(1)}, u32[]{:S(2)}, u32[]{:S(2)}) %collective-permute-start.8) | collective-permute-done | bytes 393248 | tf_op jit(solution)/shard_map/ppermute | solution.py:252
  263.1 11.9 %shard_map.223 = bf16[768,2560]{1,0:T(8,128)(2,1)} custom-call(bf16[1024,768]{1,0:T(8,128)(2,1)} %get-tuple-element.54.h1_ref, bf16[1024,768]{1,0:T(8,128)(2,1)} %get-tuple-element.55.h2_ref, bf16[1024,768]{1,0:T(8,128)(2,1)} %get-tuple-element.56.da_ref, bf16[1024,768]{1,0:T(8,128)(2,1)} %get-tuple-element.57.dqkv_ref, ...), custom_call_target="tpu_custom_call" | custom-call | flops 4000000000 | bytes 20000000 | tf_op jit(solution)/shard_map/pallas_call | solution.py:204
  275.8 1.1 copy-done.3
  277.5 3.0 add_convert_fusion.1.dy_ref
  280.4 22.7 %shard_map.224 = (bf16[1024,768]{1,0:T(8,128)(2,1)}, bf16[1024,768]{1,0:T(8,128)(2,1)}, bf16[1024,768]{1,0:T(8,128)(2,1)}, f32[8,768]{1,0:T(8,128)}, f32[8,1536]{1,0:T(8,128)}) custom-call(bf16[1024,768]{1,0:T(8,128)(2,1)} %constant_dynamic-slice_fusion.11.x_ref, bf16[1024,768]{1,0:T(8,128)(2,1)} %add_convert_fusion.1.dy_ref, ...), custom_call_target="tpu_custom_call" | custom-call | flops 8000000000 | bytes 20000000 | tf_op jit(solution)/shard_map/pallas_call | solution.py:204
  303.1 1.2 constant_dynamic-slice_fusion.4
  305.1 1.6 collective-permute-done.10
  307.3 9.3 %collective-permute-done.1 = bf16[256,768]{1,0:T(8,128)(2,1)S(1)} collective-permute-done((bf16[256,768]{1,0:T(8,128)(2,1)S(1)}, bf16[256,768]{1,0:T(8,128)(2,1)S(1)}, u32[]{:S(2)}, u32[]{:S(2)}) %collective-permute-start.1) | collective-permute-done | bytes 393248 | tf_op jit(solution)/shard_map/ppermute | solution.py:247
  317.1 7.9 %collective-permute-done.11 = bf16[256,768]{1,0:T(8,128)(2,1)S(1)} collective-permute-done((bf16[256,768]{1,0:T(8,128)(2,1)S(1)}, bf16[256,768]{1,0:T(8,128)(2,1)S(1)}, u32[]{:S(2)}, u32[]{:S(2)}) %collective-permute-start.11) | collective-permute-done | bytes 393248 | tf_op jit(solution)/shard_map/ppermute | solution.py:247
  325.6 7.9 %collective-permute-done.2 = bf16[256,768]{1,0:T(8,128)(2,1)S(1)} collective-permute-done((bf16[256,768]{1,0:T(8,128)(2,1)S(1)}, bf16[256,768]{1,0:T(8,128)(2,1)S(1)}, u32[]{:S(2)}, u32[]{:S(2)}) %collective-permute-start.2) | collective-permute-done | bytes 393248 | tf_op jit(solution)/shard_map/ppermute | solution.py:252
  333.6 0.9 pad_maximum_fusion.2
  334.5 7.0 %collective-permute-done.12 = bf16[256,768]{1,0:T(8,128)(2,1)S(1)} collective-permute-done((bf16[256,768]{1,0:T(8,128)(2,1)S(1)}, bf16[256,768]{1,0:T(8,128)(2,1)S(1)}, u32[]{:S(2)}, u32[]{:S(2)}) %collective-permute-start.12) | collective-permute-done | bytes 393248 | tf_op jit(solution)/shard_map/ppermute | solution.py:252
  341.6 0.9 pad_maximum_fusion.4
  342.5 12.3 %shard_map.225 = bf16[768,2560]{1,0:T(8,128)(2,1)} custom-call(bf16[1024,768]{1,0:T(8,128)(2,1)} %get-tuple-element.67.h1_ref, bf16[1024,768]{1,0:T(8,128)(2,1)} %get-tuple-element.68.h2_ref, bf16[1024,768]{1,0:T(8,128)(2,1)} %get-tuple-element.69.da_ref, bf16[1024,768]{1,0:T(8,128)(2,1)} %get-tuple-element.70.dqkv_ref, ...), custom_call_target="tpu_custom_call" | custom-call | flops 4000000000 | bytes 20000000 | tf_op jit(solution)/shard_map/pallas_call | solution.py:204
  354.8 1.8 broadcast_select_fusion.9
  356.6 1.2 pad_maximum_fusion.1
  357.9 1.4 copy-done.1
  359.3 4.7 collective-permute-start.15
  363.9 3.3 add_convert_fusion
  367.2 1.3 collective-permute-start.14
  368.5 1.3 collective-permute-start.4
  369.8 0.8 slice.143
  370.6 0.8 slice.142
  371.4 3.1 add_convert_fusion.2
  374.5 8.0 %collective-permute-start.5 = (bf16[1024,768]{1,0:T(8,128)(2,1)}, bf16[1024,768]{1,0:T(8,128)(2,1)}, u32[]{:S(2)}, u32[]{:S(2)}) collective-permute-start(bf16[1024,768]{1,0:T(8,128)(2,1)} %add_convert_fusion.2), channel_id=1, source_target_pairs={{0,16},{1,17},{2,18},{3,19},{4,20},{5,21},{6,22},{7,23},{8,24},{9,... | collective-permute-start | bytes 4718600 | tf_op jit(solution)/shard_map/ppermute | solution.py:345
  382.6 38.0 %psum.23 = f32[2,1536]{1,0:T(2,128)S(1)} all-reduce(f32[2,1536]{1,0:T(2,128)S(1)} %pad_maximum_fusion.6), channel_id=1, replica_groups=mesh['section'=2,'fsdp'=4,'tensor'=4] {'section','fsdp'}, use_global_device_ids=true, to_apply=%region_6.7 | all-reduce | flops 3072 | bytes 24576 | tf_op jit(solution)/shard_map/psum | solution.py:363
  420.5 0.6 constant_dynamic-slice_fusion.2
  421.1 0.6 broadcast_in_dim.50
  421.8 51.5 %psum.22 = f32[2,5,768]{2,1,0:T(8,128)S(1)} all-reduce(f32[2,5,768]{2,1,0:T(8,128)S(1)} %pad_maximum_fusion.5), channel_id=1, replica_groups=mesh['section'=2,'fsdp'=4,'tensor'=4] {'section','fsdp','tensor'}, use_global_device_ids=true, to_apply=%region_3.4 | all-reduce | flops 7680 | bytes 61440 | tf_op jit(solution)/shard_map/psum | solution.py:360
  473.3 0.7 fusion.7
  474.0 4.1 broadcast_select_fusion.1
  478.1 4.2 collective-permute-start.17
  482.3 1.3 collective-permute-start.16
  483.6 3.7 maximum_bitcast_fusion.1
  487.3 1.8 broadcast_select_fusion.5
  489.1 1.9 maximum_bitcast_fusion
  491.0 12.1 %collective-permute-done.17 = bf16[192,2560]{1,0:T(8,128)(2,1)S(1)} collective-permute-done((bf16[192,2560]{1,0:T(8,128)(2,1)}, bf16[192,2560]{1,0:T(8,128)(2,1)S(1)}, u32[]{:S(2)}, u32[]{:S(2)}) %collective-permute-start.17) | collective-permute-done | bytes 983072 | tf_op jit(solution)/shard_map/ppermute | solution.py:345
  503.0 4.1 collective-permute-done.16
  507.6 1.1 slice_bitcast_fusion.1
  509.2 0.9 copy.65
  510.1 0.8 copy.66
  (120 shorter events, 9.0 us)
Async XLA Ops:
  7.2 1.7 copy-start.10
  7.2 1.8 copy-start.20
  7.2 1.8 copy-start.19
  7.2 1.8 copy-start.18
  7.2 1.8 copy-start.17
  7.2 2.0 copy-start.8
  7.2 2.0 copy-start.9
  7.3 124.6 %all-gather.3.cloned.1.call-start = ((), (), s32[]{:S(2)}) async-start(), calls=%async_computation.2 | async-start | bytes 8847360 | tf_op jit(solution)/shard_map/all_gather | solution.py:279
  9.2 1.3 copy-start.13
  9.2 2.9 copy-start.16
  10.4 185.9 %all-reduce.5.cloned.1.call-start = ((), (), s32[]{:S(2)}) async-start(), calls=%async_computation.3 | async-start | bytes 3145728 | tf_op jit(solution)/shard_map/psum | solution.py:318
  16.0 1.8 copy-start.15
  155.1 323.0 %reduce-scatter.5.cloned.1.call-start = ((), (), s32[]{:S(2)}) async-start(), calls=%async_computation.5 | async-start | bytes 4915200 | tf_op jit(solution)/shard_map/reduce_scatter | solution.py:336
  155.7 40.6 %copy-start.2 = (bf16[2048,768]{1,0:T(8,128)(2,1)S(1)}, bf16[2048,768]{1,0:T(8,128)(2,1)}, u32[]{:S(2)}) copy-start(bf16[2048,768]{1,0:T(8,128)(2,1)} %param.13) | copy-start | bytes 9437188
  237.3 3.7 copy-start.4
  238.6 2.4 collective-permute-start.6
  241.2 11.2 %collective-permute-start.7 = (bf16[256,768]{1,0:T(8,128)(2,1)S(1)}, bf16[256,768]{1,0:T(8,128)(2,1)S(1)}, u32[]{:S(2)}, u32[]{:S(2)}) collective-permute-start(bf16[256,768]{1,0:T(8,128)(2,1)S(1)} %constant_dynamic-slice_fusion.5), channel_id=1, source_target_pairs={{0,2},{1,3},{2,0},{3,1},{4,6},{5,7},{6,4},{7,5},{8,10},{9,11},{10,... | collective-permute-start | bytes 1179656 | tf_op jit(solution)/shard_map/ppermute | solution.py:247
  252.6 10.4 %collective-permute-start.8 = (bf16[256,768]{1,0:T(8,128)(2,1)S(1)}, bf16[256,768]{1,0:T(8,128)(2,1)S(1)}, u32[]{:S(2)}, u32[]{:S(2)}) collective-permute-start(bf16[256,768]{1,0:T(8,128)(2,1)S(1)} %add_convert_fusion.8), channel_id=1, source_target_pairs={{0,2},{1,3},{2,0},{3,1},{4,6},{5,7},{6,4},{7,5},{8,10},{9,11},{10,... | collective-permute-start | bytes 1179656 | tf_op jit(solution)/shard_map/ppermute | solution.py:252
  263.1 12.0 %collective-permute-start.9 = (bf16[512,768]{1,0:T(8,128)(2,1)S(1)}, bf16[512,768]{1,0:T(8,128)(2,1)S(1)}, u32[]{:S(2)}, u32[]{:S(2)}) collective-permute-start(bf16[512,768]{1,0:T(8,128)(2,1)S(1)} %pad_maximum_fusion.3), channel_id=1, source_target_pairs={{0,1},{1,0},{2,3},{3,2},{4,5},{5,4},{6,7},{7,6},{8,9},{9,8},{10,11... | collective-permute-start | bytes 2359304 | tf_op jit(solution)/shard_map/ppermute | solution.py:252
  275.5 1.4 copy-start.3
  275.5 206.8 %reduce-scatter.3.cloned.1.call-start = ((), (), s32[]{:S(2)}) async-start(), calls=%async_computation.4 | async-start | bytes 4915200 | tf_op jit(solution)/shard_map/reduce_scatter | solution.py:338
  276.9 27.5 %collective-permute-start = (bf16[512,768]{1,0:T(8,128)(2,1)S(1)}, bf16[512,768]{1,0:T(8,128)(2,1)S(1)}, u32[]{:S(2)}, u32[]{:S(2)}) collective-permute-start(bf16[512,768]{1,0:T(8,128)(2,1)S(1)} %constant_dynamic-slice_fusion.9), channel_id=1, source_target_pairs={{0,1},{1,0},{2,3},{3,2},{4,5},{5,4},{6,7},{7,6},{8,9},{9,8},{10,11... | collective-permute-start | bytes 2359304 | tf_op jit(solution)/shard_map/ppermute | solution.py:247
  304.3 2.4 copy-start.5
  304.3 2.4 collective-permute-start.10
  304.7 12.0 %collective-permute-start.1 = (bf16[256,768]{1,0:T(8,128)(2,1)S(1)}, bf16[256,768]{1,0:T(8,128)(2,1)S(1)}, u32[]{:S(2)}, u32[]{:S(2)}) collective-permute-start(bf16[256,768]{1,0:T(8,128)(2,1)S(1)} %constant_dynamic-slice_fusion.8), channel_id=1, source_target_pairs={{0,2},{1,3},{2,0},{3,1},{4,6},{5,7},{6,4},{7,5},{8,10},{9,11},{10,... | collective-permute-start | bytes 1179656 | tf_op jit(solution)/shard_map/ppermute | solution.py:247
  306.9 18.2 %collective-permute-start.11 = (bf16[256,768]{1,0:T(8,128)(2,1)S(1)}, bf16[256,768]{1,0:T(8,128)(2,1)S(1)}, u32[]{:S(2)}, u32[]{:S(2)}) collective-permute-start(bf16[256,768]{1,0:T(8,128)(2,1)S(1)} %constant_dynamic-slice_fusion.3), channel_id=1, source_target_pairs={{0,2},{1,3},{2,0},{3,1},{4,6},{5,7},{6,4},{7,5},{8,10},{9,11},{10,... | collective-permute-start | bytes 1179656 | tf_op jit(solution)/shard_map/ppermute | solution.py:247
  316.8 16.7 %collective-permute-start.2 = (bf16[256,768]{1,0:T(8,128)(2,1)S(1)}, bf16[256,768]{1,0:T(8,128)(2,1)S(1)}, u32[]{:S(2)}, u32[]{:S(2)}) collective-permute-start(bf16[256,768]{1,0:T(8,128)(2,1)S(1)} %add_convert_fusion.9), channel_id=1, source_target_pairs={{0,2},{1,3},{2,0},{3,1},{4,6},{5,7},{6,4},{7,5},{8,10},{9,11},{10,... | collective-permute-start | bytes 1179656 | tf_op jit(solution)/shard_map/ppermute | solution.py:252
  325.2 16.3 %collective-permute-start.12 = (bf16[256,768]{1,0:T(8,128)(2,1)S(1)}, bf16[256,768]{1,0:T(8,128)(2,1)S(1)}, u32[]{:S(2)}, u32[]{:S(2)}) collective-permute-start(bf16[256,768]{1,0:T(8,128)(2,1)S(1)} %add_convert_fusion.7), channel_id=1, source_target_pairs={{0,2},{1,3},{2,0},{3,1},{4,6},{5,7},{6,4},{7,5},{8,10},{9,11},{10,... | collective-permute-start | bytes 1179656 | tf_op jit(solution)/shard_map/ppermute | solution.py:252
  334.5 20.3 %collective-permute-start.3 = (bf16[512,768]{1,0:T(8,128)(2,1)}, bf16[512,768]{1,0:T(8,128)(2,1)S(1)}, u32[]{:S(2)}, u32[]{:S(2)}) collective-permute-start(bf16[512,768]{1,0:T(8,128)(2,1)} %pad_maximum_fusion.2), channel_id=1, source_target_pairs={{0,1},{1,0},{2,3},{3,2},{4,5},{5,4},{6,7},{7,6},{8,9},{9,8},{10,11... | collective-permute-start | bytes 2359304 | tf_op jit(solution)/shard_map/ppermute | solution.py:252
  342.5 12.3 %collective-permute-start.13 = (bf16[512,768]{1,0:T(8,128)(2,1)}, bf16[512,768]{1,0:T(8,128)(2,1)S(1)}, u32[]{:S(2)}, u32[]{:S(2)}) collective-permute-start(bf16[512,768]{1,0:T(8,128)(2,1)} %pad_maximum_fusion.4), channel_id=1, source_target_pairs={{0,1},{1,0},{2,3},{3,2},{4,5},{5,4},{6,7},{7,6},{8,9},{9,8},{10,11... | collective-permute-start | bytes 2359304 | tf_op jit(solution)/shard_map/ppermute | solution.py:252
  357.8 1.4 copy-start.1
  359.3 9.2 %copy-start = (bf16[1024,768]{1,0:T(8,128)(2,1)S(1)}, bf16[1024,768]{1,0:T(8,128)(2,1)}, u32[]{:S(2)}) copy-start(bf16[1024,768]{1,0:T(8,128)(2,1)} %add_convert_fusion.3.x_ref) | copy-start | bytes 4718596
  359.3 114.7 %collective-permute-start.15 = (bf16[1024,768]{1,0:T(8,128)(2,1)S(1)}, bf16[1024,768]{1,0:T(8,128)(2,1)}, u32[]{:S(2)}, u32[]{:S(2)}) collective-permute-start(bf16[1024,768]{1,0:T(8,128)(2,1)S(1)} %copy-done.1), channel_id=1, source_target_pairs={{0,16},{1,17},{2,18},{3,19},{4,20},{5,21},{6,22},{7,23},{8,24},{9,... | collective-permute-start | bytes 4718600 | tf_op jit(solution)/shard_map/ppermute | solution.py:345
  367.2 106.8 %collective-permute-start.14 = (bf16[1024,768]{1,0:T(8,128)(2,1)}, bf16[1024,768]{1,0:T(8,128)(2,1)}, u32[]{:S(2)}, u32[]{:S(2)}) collective-permute-start(bf16[1024,768]{1,0:T(8,128)(2,1)} %add_convert_fusion), channel_id=1, source_target_pairs={{16,0},{17,1},{18,2},{19,3},{20,4},{21,5},{22,6},{23,7},{24,8},{25... | collective-permute-start | bytes 4718600 | tf_op jit(solution)/shard_map/ppermute | solution.py:344
  368.5 118.8 %collective-permute-start.4 = (bf16[1024,768]{1,0:T(8,128)(2,1)S(1)}, bf16[1024,768]{1,0:T(8,128)(2,1)}, u32[]{:S(2)}, u32[]{:S(2)}) collective-permute-start(bf16[1024,768]{1,0:T(8,128)(2,1)S(1)} %copy-done), channel_id=1, source_target_pairs={{16,0},{17,1},{18,2},{19,3},{20,4},{21,5},{22,6},{23,7},{24,8},{25... | collective-permute-start | bytes 4718600 | tf_op jit(solution)/shard_map/ppermute | solution.py:344
  371.4 50.3 %copy-start.11 = (f32[8,768]{1,0:T(8,128)S(1)}, f32[8,768]{1,0:T(8,128)}, u32[]{:S(2)}) copy-start(f32[8,768]{1,0:T(8,128)} %get-tuple-element.75) | copy-start | bytes 73732
  371.4 50.3 %copy-start.12 = (f32[8,768]{1,0:T(8,128)S(1)}, f32[8,768]{1,0:T(8,128)}, u32[]{:S(2)}) copy-start(f32[8,768]{1,0:T(8,128)} %get-tuple-element.74) | copy-start | bytes 73732
  374.5 112.8 %collective-permute-start.5 = (bf16[1024,768]{1,0:T(8,128)(2,1)}, bf16[1024,768]{1,0:T(8,128)(2,1)}, u32[]{:S(2)}, u32[]{:S(2)}) collective-permute-start(bf16[1024,768]{1,0:T(8,128)(2,1)} %add_convert_fusion.2), channel_id=1, source_target_pairs={{0,16},{1,17},{2,18},{3,19},{4,20},{5,21},{6,22},{7,23},{8,24},{9,... | collective-permute-start | bytes 4718600 | tf_op jit(solution)/shard_map/ppermute | solution.py:345
  473.3 37.6 %copy-start.14 = (f32[1,192]{1,0:T(1,128)}, f32[1,192]{1,0:T(1,128)S(1)}, u32[]{:S(2)}) copy-start(f32[1,192]{1,0:T(1,128)S(1)} %dynamic-slice_bitcast_fusion) | copy-start | bytes 2308
  478.1 25.0 %collective-permute-start.17 = (bf16[192,2560]{1,0:T(8,128)(2,1)}, bf16[192,2560]{1,0:T(8,128)(2,1)S(1)}, u32[]{:S(2)}, u32[]{:S(2)}) collective-permute-start(bf16[192,2560]{1,0:T(8,128)(2,1)} %reduce-scatter.5.cloned.1.call-done), channel_id=1, source_target_pairs={{0,16},{1,17},{2,18},{3,19},{4,20},{5,21},{6,22},{7,23},{8,24},{9,... | collective-permute-start | bytes 2949128 | tf_op jit(solution)/shard_map/ppermute | solution.py:345
  482.3 24.9 %collective-permute-start.16 = (bf16[192,2560]{1,0:T(8,128)(2,1)}, bf16[192,2560]{1,0:T(8,128)(2,1)S(1)}, u32[]{:S(2)}, u32[]{:S(2)}) collective-permute-start(bf16[192,2560]{1,0:T(8,128)(2,1)} %reduce-scatter.3.cloned.1.call-done), channel_id=1, source_target_pairs={{16,0},{17,1},{18,2},{19,3},{20,4},{21,5},{22,6},{23,7},{24,8},{25... | collective-permute-start | bytes 2949128 | tf_op jit(solution)/shard_map/ppermute | solution.py:344
  489.1 18.1 %copy-start.6 = (bf16[192,2560]{1,0:T(8,128)(2,1)S(1)}, bf16[192,2560]{1,0:T(8,128)(2,1)}, u32[]{:S(2)}) copy-start(bf16[192,2560]{1,0:T(8,128)(2,1)} %reduce-scatter.5.cloned.1.call-done) | copy-start | bytes 2949124
  489.1 18.1 %copy-start.7 = (bf16[192,2560]{1,0:T(8,128)(2,1)S(1)}, bf16[192,2560]{1,0:T(8,128)(2,1)}, u32[]{:S(2)}) copy-start(bf16[192,2560]{1,0:T(8,128)(2,1)} %reduce-scatter.3.cloned.1.call-done) | copy-start | bytes 2949124
Sparse Core Ops, SparseCore 0:
  10.8 121.0 all-gather.2
  155.2 41.0 all-reduce.4
  275.6 72.8 reduce-scatter.4
  358.0 73.8 reduce-scatter.2
